TPU v7x, 32 devices: a whole 2x2x4 slice. The times are simulated.
32 devices in a mesh: dp: 8 (over y, x, core), tensor: 4 (over z).
Axes of the slice: x: 2, y: 2, z: 4, core: 2. Of those that a mesh axis runs over, the one named last changes fastest.
Arguments:
- tokens: bfloat16 [2, 1024, 1536], P(None, 'dp'), may hold values from -6 to 6
- context: bfloat16 [2, 48, 1024], P(None, 'dp'), may hold values from -6 to 6
- captions: bfloat16 [2, 48, 256, 4096], P(None, 'dp'), may hold values from -6 to 6
- shapes: int32 [2, 48, 2], P(None, 'dp'), may hold values from 0 to 31, as said below
- text_len: int32 [2, 48], P(None, 'dp'), may hold values from 32 to 256, as said below
- w_query: bfloat16 [1536, 1536], P('dp', 'tensor'), may hold values from -0.15625 to 0.15625
- w_key: bfloat16 [1536, 1536], P('dp', 'tensor'), may hold values from -0.15625 to 0.15625
- w_value: bfloat16 [1536, 1536], P('dp', 'tensor'), may hold values from -0.15625 to 0.15625
- w_out: bfloat16 [1536, 1536], P('dp', 'tensor'), may hold values from -0.625 to 0.625
- w_text_key: bfloat16 [4096, 1536], P('dp', 'tensor'), may hold values from -0.09375 to 0.09375
- w_text_value: bfloat16 [4096, 1536], P('dp', 'tensor'), may hold values from -0.09375 to 0.09375
- w_gate: bfloat16 [1536, 4096], P('dp', 'tensor'), may hold values from -0.15625 to 0.15625
- w_up: bfloat16 [1536, 4096], P('dp', 'tensor'), may hold values from -0.15625 to 0.15625
- w_down: bfloat16 [1536, 4096], P('dp', 'tensor'), may hold values from -0.1875 to 0.1875
- w_adaln: bfloat16 [1024, 6144], P('dp', 'tensor'), may hold values from -0.25 to 0.25
- gain_attn: bfloat16 [1536], P('dp'), may hold values from 0.25 to 1.75
- gain_ffn: bfloat16 [1536], P('dp'), may hold values from 0.25 to 1.75
- gain_query: bfloat16 [64, 24], P('dp', 'tensor'), may hold values from 0.25 to 1.75
- gain_key: bfloat16 [64, 24], P('dp', 'tensor'), may hold values from 0.25 to 1.75
- gain_text: bfloat16 [64, 24], P('dp', 'tensor'), may hold values from 0.25 to 1.75
- cross_gate: bfloat16 [24], P('tensor'), may hold values from -1.5 to 1.5
- cotangent: bfloat16 [2, 1024, 1536], P(None, 'dp'), may hold values from -6 to 6
Outputs:
- result: bfloat16 [2, 1024, 1536], P(None, 'dp')
- grad_tokens: bfloat16 [2, 1024, 1536], P(None, 'dp')
- grad_w_query: float32 [1536, 1536], P('dp', 'tensor')
- grad_w_key: float32 [1536, 1536], P('dp', 'tensor')
- grad_w_value: float32 [1536, 1536], P('dp', 'tensor')
- grad_w_out: float32 [1536, 1536], P('dp', 'tensor')
- grad_w_text_key: float32 [4096, 1536], P('dp', 'tensor')
- grad_w_text_value: float32 [4096, 1536], P('dp', 'tensor')
- grad_w_gate: float32 [1536, 4096], P('dp', 'tensor')
- grad_w_up: float32 [1536, 4096], P('dp', 'tensor')
- grad_w_down: float32 [1536, 4096], P('dp', 'tensor')
- grad_w_adaln: float32 [1024, 6144], P('dp', 'tensor')
- grad_gain_attn: float32 [1536], P('dp')
- grad_gain_ffn: float32 [1536], P('dp')
- grad_gain_query: float32 [64, 24], P('dp', 'tensor')
- grad_gain_key: float32 [64, 24], P('dp', 'tensor')
- grad_gain_text: float32 [64, 24], P('dp', 'tensor')
- grad_cross_gate: float32 [24], P('tensor')
Inputs may be any that keep to these rules, and one draw needn't show every extreme that they name: `shapes`: each slot holds an image of rows x (cols + 1) tokens (cols patch columns and one line-end token per row), packed in slot order from the first token of its device's micro-batch rows; an empty slot has rows = cols = 0, otherwise rows is 2 to 4 and cols 7 to 31. The first slot of each device is never empty; the images of one device in one micro-batch take at most 128 tokens, and in each micro-batch one device is filled exactly by one image of 4 rows and 31 columns. `text_len`: in each micro-batch some slot has all 256 caption tokens live.
All inputs are finite; a program needn't handle non-finite values.
Results may differ from a plain program's by a relative error of at most 0.035.
Values may be sent and summed in bfloat16 or wider, within the bound.
A program may use at most 256 MiB of HBM per device.

v0:
```python
import jax
import jax.numpy as jnp
from jax import lax
from jax.sharding import PartitionSpec as P

HEAD_DIM = 64
DT = 4096
TXT = 256


EPSILON = 1e-06
MASKED = -1e30
ROPE_BASE = 10000.0


def image_layout(shapes, count):
    height = shapes[:, 0]
    stride_all = shapes[:, 1] + 1
    extent = height * stride_all
    finish = jnp.cumsum(extent)
    begin = finish - extent
    places = jnp.arange(count, dtype=jnp.int32)
    member = (places[:, None] >= begin[None, :]) & (places[:, None] < finish[None, :])
    member_int = member.astype(jnp.int32)
    inside = jnp.sum(member_int, axis=1)
    slot_ids = jnp.arange(shapes.shape[0], dtype=jnp.int32)
    segment = jnp.sum(member_int * slot_ids[None, :], axis=1)
    stride = jnp.sum(member_int * stride_all[None, :], axis=1) + 1 - inside
    offset = places - jnp.sum(member_int * begin[None, :], axis=1)
    return (member.astype(jnp.float32), segment, inside, offset // stride, offset % stride)


def rope_tables(row_pos, col_pos):
    quarter = HEAD_DIM // 4
    freq = ROPE_BASE ** (-jnp.arange(quarter, dtype=jnp.float32) / quarter)
    angles = jnp.stack(
        [
            row_pos.astype(jnp.float32)[:, None] * freq[None, :],
            col_pos.astype(jnp.float32)[:, None] * freq[None, :],
        ],
        axis=1,
    )
    return (jnp.cos(angles), jnp.sin(angles))


def rotate(values, cosine_table, sine_table):
    count, heads, width = values.shape
    parts = values.reshape(count, heads, 2, 2, width // 4)
    former = parts[:, :, :, 0, :]
    latter = parts[:, :, :, 1, :]
    cos_wide = cosine_table[:, None, :, :]
    sin_wide = sine_table[:, None, :, :]
    turned = jnp.stack(
        [former * cos_wide - latter * sin_wide, latter * cos_wide + former * sin_wide], axis=3
    )
    return turned.reshape(count, heads, width)


def head_norm(values, gain):
    scale = lax.rsqrt(jnp.mean(values * values, axis=-1, keepdims=True) + EPSILON)
    return values * scale * gain.T[None, :, :]


def modulate(values, gain, scale):
    normed = values * lax.rsqrt(jnp.mean(values * values, axis=1, keepdims=True) + EPSILON)
    return normed * gain * (1.0 + scale)


def activate(gate_val, up_val):
    return jax.nn.silu(gate_val) * up_val


def contract_rows(left, right):
    return lax.dot_general(
        left, right, (((0,), (0,)), ((), ())), preferred_element_type=jnp.float32
    )


def contract_cols(left, right):
    return lax.dot_general(
        left, right, (((1,), (1,)), ((), ())), preferred_element_type=jnp.float32
    )


def score_block(queries, keys, allowed, scale):
    scores = jnp.einsum("thd,shd->hts", queries, keys, preferred_element_type=jnp.float32) * scale
    return jnp.where(allowed[None], scores, MASKED)


def attend_forward(queries, keys, values, allowed, scale):
    scores = score_block(queries, keys, allowed, scale)
    peak = jnp.max(scores, axis=2, keepdims=True)
    expo = jnp.exp(scores - peak)
    total = jnp.sum(expo, axis=2, keepdims=True)
    probs = (expo / total).astype(jnp.bfloat16)
    output = jnp.einsum("hts,shd->thd", probs, values, preferred_element_type=jnp.float32)
    return (output, peak + jnp.log(total))


def attend_backward(queries, keys, values, allowed, scale, log_total, grad_out):
    probs = jnp.exp(score_block(queries, keys, allowed, scale) - log_total)
    grad_probs = jnp.einsum("thd,shd->hts", grad_out, values, preferred_element_type=jnp.float32)
    grad_scores = probs * (grad_probs - jnp.sum(probs * grad_probs, axis=2, keepdims=True))
    scaled = (grad_scores * scale).astype(jnp.bfloat16)
    grad_query = jnp.einsum("hts,shd->thd", scaled, keys, preferred_element_type=jnp.float32)
    grad_key = jnp.einsum("hts,thd->shd", scaled, queries, preferred_element_type=jnp.float32)
    grad_value = jnp.einsum(
        "hts,thd->shd", probs.astype(jnp.bfloat16), grad_out, preferred_element_type=jnp.float32
    )
    return (grad_query, grad_key, grad_value)


def share_each(grads):
    return (
        lax.psum_scatter(grads[0], "dp", scatter_dimension=0, tiled=True),
        lax.psum_scatter(grads[1], "dp", scatter_dimension=0, tiled=True),
        lax.psum_scatter(grads[2], "dp", scatter_dimension=0, tiled=True),
        lax.psum_scatter(grads[3], "dp", scatter_dimension=0, tiled=True),
        lax.psum_scatter(grads[4], "dp", scatter_dimension=0, tiled=True),
        lax.psum_scatter(grads[5], "dp", scatter_dimension=0, tiled=True),
        lax.psum_scatter(grads[6], "dp", scatter_dimension=0, tiled=True),
        lax.psum_scatter(grads[7], "dp", scatter_dimension=0, tiled=True),
        lax.psum_scatter(grads[8], "dp", scatter_dimension=0, tiled=True),
        lax.psum_scatter(grads[9], "dp", scatter_dimension=0, tiled=True),
        lax.psum_scatter(grads[10], "dp", scatter_dimension=0, tiled=True),
        lax.psum_scatter(grads[11], "dp", scatter_dimension=0, tiled=True),
        lax.psum_scatter(grads[12], "dp", scatter_dimension=0, tiled=True),
        lax.psum_scatter(grads[13], "dp", scatter_dimension=0, tiled=True),
        lax.psum_scatter(grads[14], "dp", scatter_dimension=0, tiled=True),
    )


def zero_like(array):
    return jnp.zeros(array.shape, jnp.float32)


def shards(
    tokens,
    context,
    captions,
    shapes,
    text_len,
    w_query,
    w_key,
    w_value,
    w_out,
    w_text_key,
    w_text_value,
    w_gate,
    w_up,
    w_down,
    w_adaln,
    gain_attn,
    gain_ffn,
    gain_query,
    gain_key,
    gain_text,
    cross_gate,
    cotangent,
):
    weights = (
        w_query,
        w_key,
        w_value,
        w_out,
        w_text_key,
        w_text_value,
        w_gate,
        w_up,
        w_down,
        w_adaln,
        gain_attn,
        gain_ffn,
        gain_query,
        gain_key,
        gain_text,
    )
    micro_count, count, width = tokens.shape
    slots = shapes.shape[1]
    local_heads = w_query.shape[1] // HEAD_DIM
    scale = HEAD_DIM ** (-0.5)
    span = w_adaln.shape[1]
    tensor_rank = lax.axis_index("tensor")
    shard_totals = jax.tree.map(zero_like, weights)
    gate_total = jnp.zeros(cross_gate.shape, jnp.float32)
    gate_tanh = jnp.tanh(cross_gate.astype(jnp.float32))[None, :, None]
    outputs = []
    tok_grads = []
    for batch_index in range(micro_count):
        gathered = (
            lax.all_gather(w_query, "dp", axis=0, tiled=True),
            lax.all_gather(w_key, "dp", axis=0, tiled=True),
            lax.all_gather(w_value, "dp", axis=0, tiled=True),
            lax.all_gather(w_out, "dp", axis=0, tiled=True),
            lax.all_gather(w_text_key, "dp", axis=0, tiled=True),
            lax.all_gather(w_text_value, "dp", axis=0, tiled=True),
            lax.all_gather(w_gate, "dp", axis=0, tiled=True),
            lax.all_gather(w_up, "dp", axis=0, tiled=True),
            lax.all_gather(w_down, "dp", axis=0, tiled=True),
            lax.all_gather(w_adaln, "dp", axis=0, tiled=True),
            lax.all_gather(gain_attn, "dp", axis=0, tiled=True),
            lax.all_gather(gain_ffn, "dp", axis=0, tiled=True),
            lax.all_gather(gain_query, "dp", axis=0, tiled=True),
            lax.all_gather(gain_key, "dp", axis=0, tiled=True),
            lax.all_gather(gain_text, "dp", axis=0, tiled=True),
        )
        (
            query_mat,
            key_mat,
            value_mat,
            out_mat,
            text_key_mat,
            text_value_mat,
            gate_mat,
            up_mat,
            down_mat,
            adaln_mat,
            attn_gain,
            ffn_gain,
            query_gain,
            key_gain,
            text_gain,
        ) = gathered
        member, segment, inside, row_pos, col_pos = image_layout(shapes[batch_index], count)
        cosine_table, sine_table = rope_tables(row_pos, col_pos)
        cond_act = jax.nn.silu(context[batch_index].astype(jnp.float32)).astype(jnp.bfloat16)
        mod_part = jnp.dot(cond_act, adaln_mat, preferred_element_type=jnp.float32)
        modulation = lax.all_gather(
            mod_part.astype(jnp.bfloat16), "tensor", axis=1, tiled=True
        ).astype(mod_part.dtype)
        token_mod = jnp.dot(member, modulation, precision=lax.Precision.HIGHEST)
        scale_attn, gate_attn, scale_ffn, gate_ffn = jnp.split(token_mod, 4, axis=1)
        residual_in = tokens[batch_index].astype(jnp.float32)
        attn_in_f, norm_pull = jax.vjp(
            modulate, residual_in, attn_gain.astype(jnp.float32), scale_attn
        )
        attn_in = attn_in_f.astype(jnp.bfloat16)

        def prep_pos(values, gain):
            return rotate(head_norm(values, gain), cosine_table, sine_table)

        query_raw = jnp.dot(attn_in, query_mat, preferred_element_type=jnp.float32)
        query_rot_f, query_pull = jax.vjp(
            prep_pos,
            query_raw.reshape(count, local_heads, HEAD_DIM),
            query_gain.astype(jnp.float32),
        )
        query_rot = query_rot_f.astype(jnp.bfloat16)
        key_raw = jnp.dot(attn_in, key_mat, preferred_element_type=jnp.float32)
        key_rot_f, key_pull = jax.vjp(
            prep_pos, key_raw.reshape(count, local_heads, HEAD_DIM), key_gain.astype(jnp.float32)
        )
        key_rot = key_rot_f.astype(jnp.bfloat16)
        value_proj = (
            jnp.dot(attn_in, value_mat, preferred_element_type=jnp.float32)
            .astype(jnp.bfloat16)
            .reshape(count, local_heads, HEAD_DIM)
        )
        text_flat = captions[batch_index].reshape(slots * TXT, DT)
        text_raw = jnp.dot(text_flat, text_key_mat, preferred_element_type=jnp.float32)
        text_key_f, text_pull = jax.vjp(
            head_norm,
            text_raw.reshape(slots * TXT, local_heads, HEAD_DIM),
            text_gain.astype(jnp.float32),
        )
        text_key = text_key_f.astype(jnp.bfloat16)
        text_value = (
            jnp.dot(text_flat, text_value_mat, preferred_element_type=jnp.float32)
            .astype(jnp.bfloat16)
            .reshape(slots * TXT, local_heads, HEAD_DIM)
        )
        self_id = jnp.where(inside > 0, segment, slots)
        self_mask = self_id[:, None] == self_id[None, :]
        key_slot = jnp.arange(slots * TXT, dtype=jnp.int32) // TXT
        text_live = (
            jnp.arange(TXT, dtype=jnp.int32)[None, :] < text_len[batch_index][:, None]
        ).reshape(slots * TXT)
        cross_mask = (segment[:, None] == key_slot[None, :]) & text_live[None, :]
        self_out, self_lse = attend_forward(query_rot, key_rot, value_proj, self_mask, scale)
        cross_out, cross_lse = attend_forward(query_rot, text_key, text_value, cross_mask, scale)
        mixed = (self_out + gate_tanh * cross_out).reshape(count, -1).astype(jnp.bfloat16)
        attn_out = lax.psum(contract_cols(mixed, out_mat).astype(jnp.bfloat16), "tensor").astype(
            jnp.float32
        )
        hidden = residual_in + jnp.tanh(gate_attn) * attn_out
        ffn_in_f, ffn_pull = jax.vjp(modulate, hidden, ffn_gain.astype(jnp.float32), scale_ffn)
        ffn_in = ffn_in_f.astype(jnp.bfloat16)
        gate_proj = jnp.dot(ffn_in, gate_mat, preferred_element_type=jnp.float32)
        up_proj = jnp.dot(ffn_in, up_mat, preferred_element_type=jnp.float32)
        inner_f, act_pull = jax.vjp(activate, gate_proj, up_proj)
        inner = inner_f.astype(jnp.bfloat16)
        ffn_out = lax.psum(contract_cols(inner, down_mat).astype(jnp.bfloat16), "tensor").astype(
            jnp.float32
        )
        outputs.append((hidden + jnp.tanh(gate_ffn) * ffn_out).astype(jnp.bfloat16))
        again = (
            lax.all_gather(w_query, "dp", axis=0, tiled=True),
            lax.all_gather(w_key, "dp", axis=0, tiled=True),
            lax.all_gather(w_value, "dp", axis=0, tiled=True),
            lax.all_gather(w_out, "dp", axis=0, tiled=True),
            lax.all_gather(w_text_key, "dp", axis=0, tiled=True),
            lax.all_gather(w_text_value, "dp", axis=0, tiled=True),
            lax.all_gather(w_gate, "dp", axis=0, tiled=True),
            lax.all_gather(w_up, "dp", axis=0, tiled=True),
            lax.all_gather(w_down, "dp", axis=0, tiled=True),
            lax.all_gather(w_adaln, "dp", axis=0, tiled=True),
            lax.all_gather(gain_attn, "dp", axis=0, tiled=True),
            lax.all_gather(gain_ffn, "dp", axis=0, tiled=True),
            lax.all_gather(gain_query, "dp", axis=0, tiled=True),
            lax.all_gather(gain_key, "dp", axis=0, tiled=True),
            lax.all_gather(gain_text, "dp", axis=0, tiled=True),
        )
        (
            query_mat,
            key_mat,
            value_mat,
            out_mat,
            text_key_mat,
            text_value_mat,
            gate_mat,
            up_mat,
            down_mat,
        ) = again[:9]
        grad_y = cotangent[batch_index].astype(jnp.float32)
        tanh_ffn = jnp.tanh(gate_ffn)
        grad_ffn_out = (tanh_ffn * grad_y).astype(jnp.bfloat16)
        grad_gate_ffn = grad_y * ffn_out * (1.0 - tanh_ffn * tanh_ffn)
        grad_inner = jnp.dot(grad_ffn_out, down_mat, preferred_element_type=jnp.float32)
        grad_down = contract_rows(grad_ffn_out, inner)
        grad_gate_f, grad_up_f = act_pull(grad_inner)
        grad_gate_b = grad_gate_f.astype(jnp.bfloat16)
        grad_up_b = grad_up_f.astype(jnp.bfloat16)
        grad_w_gate = contract_rows(ffn_in, grad_gate_b)
        grad_w_up = contract_rows(ffn_in, grad_up_b)
        ffn_part = contract_cols(grad_gate_b, gate_mat) + contract_cols(grad_up_b, up_mat)
        grad_ffn_in = lax.psum(ffn_part.astype(jnp.bfloat16), "tensor").astype(jnp.float32)
        grad_hidden_norm, grad_ffn_gain, grad_scale_ffn = ffn_pull(grad_ffn_in)
        grad_hidden = grad_y + grad_hidden_norm
        tanh_attn = jnp.tanh(gate_attn)
        grad_attn_out = (tanh_attn * grad_hidden).astype(jnp.bfloat16)
        grad_gate_attn = grad_hidden * attn_out * (1.0 - tanh_attn * tanh_attn)
        grad_mixed = jnp.dot(grad_attn_out, out_mat, preferred_element_type=jnp.float32).reshape(
            count, local_heads, HEAD_DIM
        )
        grad_w_out = contract_rows(grad_attn_out, mixed)
        grad_self = grad_mixed.astype(jnp.bfloat16)
        grad_cross = (gate_tanh * grad_mixed).astype(jnp.bfloat16)
        gate_total = gate_total + jnp.sum(grad_mixed * cross_out, axis=(0, 2)) * (
            1.0 - gate_tanh[0, :, 0] * gate_tanh[0, :, 0]
        )
        grad_q_self, grad_k_self, grad_v_self = attend_backward(
            query_rot, key_rot, value_proj, self_mask, scale, self_lse, grad_self
        )
        grad_q_cross, grad_k_text, grad_v_text = attend_backward(
            query_rot, text_key, text_value, cross_mask, scale, cross_lse, grad_cross
        )
        grad_query_raw, grad_query_gain = query_pull(grad_q_self + grad_q_cross)
        grad_key_raw, grad_key_gain = key_pull(grad_k_self)
        grad_text_raw, grad_text_gain = text_pull(grad_k_text)
        grad_query_b = grad_query_raw.reshape(count, -1).astype(jnp.bfloat16)
        grad_key_b = grad_key_raw.reshape(count, -1).astype(jnp.bfloat16)
        grad_value_b = grad_v_self.reshape(count, -1).astype(jnp.bfloat16)
        grad_text_key_b = grad_text_raw.reshape(slots * TXT, -1).astype(jnp.bfloat16)
        grad_text_value_b = grad_v_text.reshape(slots * TXT, -1).astype(jnp.bfloat16)
        attn_part = (
            contract_cols(grad_query_b, query_mat)
            + contract_cols(grad_key_b, key_mat)
            + contract_cols(grad_value_b, value_mat)
        )
        grad_attn_in = lax.psum(attn_part.astype(jnp.bfloat16), "tensor").astype(jnp.float32)
        grad_resid_norm, grad_attn_gain, grad_scale_attn = norm_pull(grad_attn_in)
        tok_grads.append((grad_hidden + grad_resid_norm).astype(jnp.bfloat16))
        grad_token_mod = jnp.concatenate(
            [grad_scale_attn, grad_gate_attn, grad_scale_ffn, grad_gate_ffn], axis=1
        )
        grad_modulation = jnp.dot(member.T, grad_token_mod, precision=lax.Precision.HIGHEST)
        grad_mod_part = lax.dynamic_slice_in_dim(
            grad_modulation, tensor_rank * span, span, 1
        ).astype(jnp.bfloat16)
        batch_grads = (
            contract_rows(attn_in, grad_query_b),
            contract_rows(attn_in, grad_key_b),
            contract_rows(attn_in, grad_value_b),
            grad_w_out,
            contract_rows(text_flat, grad_text_key_b),
            contract_rows(text_flat, grad_text_value_b),
            grad_w_gate,
            grad_w_up,
            grad_down,
            contract_rows(cond_act, grad_mod_part),
            grad_attn_gain,
            grad_ffn_gain,
            grad_query_gain,
            grad_key_gain,
            grad_text_gain,
        )
        shard_totals = jax.tree.map(jnp.add, shard_totals, share_each(batch_grads))
    gate_grad = lax.psum(gate_total, "dp")
    return (
        jnp.stack(outputs, axis=0),
        jnp.stack(tok_grads, axis=0),
        shard_totals[0],
        shard_totals[1],
        shard_totals[2],
        shard_totals[3],
        shard_totals[4],
        shard_totals[5],
        shard_totals[6],
        shard_totals[7],
        shard_totals[8],
        shard_totals[9],
        shard_totals[10],
        shard_totals[11],
        shard_totals[12],
        shard_totals[13],
        shard_totals[14],
        gate_grad,
    )


def solution(mesh):
    return jax.shard_map(
        shards,
        mesh=mesh,
        in_specs=(
            P(None, "dp", None),
            P(None, "dp", None),
            P(None, "dp", None, None),
            P(None, "dp", None),
            P(None, "dp"),
            P("dp", "tensor"),
            P("dp", "tensor"),
            P("dp", "tensor"),
            P("dp", "tensor"),
            P("dp", "tensor"),
            P("dp", "tensor"),
            P("dp", "tensor"),
            P("dp", "tensor"),
            P("dp", "tensor"),
            P("dp", "tensor"),
            P("dp"),
            P("dp"),
            P("dp", "tensor"),
            P("dp", "tensor"),
            P("dp", "tensor"),
            P("tensor"),
            P(None, "dp", None),
        ),
        out_specs=(
            P(None, "dp", None),
            P(None, "dp", None),
            P("dp", "tensor"),
            P("dp", "tensor"),
            P("dp", "tensor"),
            P("dp", "tensor"),
            P("dp", "tensor"),
            P("dp", "tensor"),
            P("dp", "tensor"),
            P("dp", "tensor"),
            P("dp", "tensor"),
            P("dp", "tensor"),
            P("dp"),
            P("dp"),
            P("dp", "tensor"),
            P("dp", "tensor"),
            P("dp", "tensor"),
            P("tensor"),
        ),
        check_vma=False,
    )
```

profile of v0, /device:TPU:8, one launch (start us, length us, event | category | flops | bytes accessed | tf_op | source)
XLA Modules:
  0.0 1226.0 jit_solution(2917586888475523133)
XLA Ops:
  17.6 14.9 %all-reduce.16 = (bf16[1536]{0:T(1024)(128)(2,1)S(1)}, bf16[1536]{0:T(1024)(128)(2,1)}) all-reduce(bf16[1536]{0:T(1024)(128)(2,1)S(1)} %dynamic-update-slice, bf16[1536]{0:T(1024)(128)(2,1)S(1)} %dynamic-update-slice.1), channel_id=1, replica_groups=mesh['dp'=8,'tensor'=4] {'dp'}, use_global_device_ids=true, to_apply=%add.8 | all-reduce | flops 3072 | bytes 12288
  43.8 8.7 all_gather.39
  54.8 17.5 %fusion.255 = (bf16[1,6,256,4096]{3,2,1,0:T(8,128)(2,1)}, bf16[1,6,256,4096]{3,2,1,0:T(8,128)(2,1)}) fusion(bf16[2,6,256,4096]{3,2,1,0:T(8,128)(2,1)} %param.24), kind=kLoop, calls=%fused_computation.479 | loop fusion | bytes 50331648 | tf_op jit(solution)/shard_map/slice | solution.py:259
  88.3 13.4 %all_gather.35 = bf16[6,6144]{1,0:T(8,128)(2,1)S(1)} all-gather(bf16[6,1536]{1,0:T(8,128)(2,1)S(1)} %convolution_convert_fusion.9), channel_id=1, replica_groups=mesh['dp'=8,'tensor'=4] {'tensor'}, dimensions={1}, use_global_device_ids=true | all-gather | bytes 92160 | tf_op jit(solution)/shard_map/all_gather | solution.py:228
  103.0 13.4 %all_gather.96 = bf16[6,6144]{1,0:T(8,128)(2,1)S(1)} all-gather(bf16[6,1536]{1,0:T(8,128)(2,1)S(1)} %convolution_convert_fusion.8), channel_id=1, replica_groups=mesh['dp'=8,'tensor'=4] {'tensor'}, dimensions={1}, use_global_device_ids=true | all-gather | bytes 92160 | tf_op jit(solution)/shard_map/all_gather | solution.py:228
  147.0 8.6 all-gather.21.cloned.1.call-done
  160.8 15.7 %multiply_reduce_fusion.6 = (f32[1536,6]{0,1:T(8,128)}, f32[1536,6,64]{0,2,1:T(8,128)}) fusion(bf16[1536,4096,1]{1,0,2:T(8,128)(2,1)} %bitcast.344, bf16[6,64,4096]{2,1,0:T(8,128)(2,1)} %bitcast.381), kind=kOutput, calls=%fused_computation.87 | convolution fusion | flops 4833008640 | bytes 18124800 | tf_op jit(solution)/shard_map/dot_general | solution.py:260
  176.5 10.9 multiply_reduce_fusion.7
  202.5 9.2 convolution_convert_fusion.2
  219.0 8.3 convolution_convert_fusion.3
  244.2 34.5 %all-reduce.28.cloned.1.call-done = (bf16[128,1536]{1,0:T(8,128)(2,1)}, bf16[128,1536]{1,0:T(8,128)(2,1)}) async-done(((bf16[128,1536]{1,0:T(8,128)(2,1)}, bf16[128,1536]{1,0:T(8,128)(2,1)}), (bf16[128,1536]{1,0:T(8,128)(2,1)}, bf16[128,1536]{1,0:T(8,128)(2,1)})) %all-reduce.28.cloned.1.call-update) | async-done | bytes 786448 | tf_op jit(solution)/shard_map/psum | solution.py:282
  284.1 28.5 %all-gather.25.cloned.1.call-done = bf16[1536,1024]{1,0:T(8,128)(2,1)} async-done(((bf16[192,1024]{1,0:T(8,128)(2,1)}), bf16[1536,1024]{1,0:T(8,128)(2,1)}) %all-gather.25.cloned.1.call-update) | async-done | bytes 3145744 | tf_op jit(solution)/shard_map/all_gather | solution.py:197
  316.0 30.7 %all-gather.27.cloned.1.call-done = bf16[1536,1024]{1,0:T(8,128)(2,1)} async-done(((bf16[192,1024]{1,0:T(8,128)(2,1)}), bf16[1536,1024]{1,0:T(8,128)(2,1)}) %all-gather.27.cloned.1.call-update) | async-done | bytes 3145744 | tf_op jit(solution)/shard_map/all_gather | solution.py:198
  354.8 26.1 %all-gather.29.cloned.1.call-done = bf16[1536,1024]{1,0:T(8,128)(2,1)} async-done(((bf16[192,1024]{1,0:T(8,128)(2,1)}), bf16[1536,1024]{1,0:T(8,128)(2,1)}) %all-gather.29.cloned.1.call-update) | async-done | bytes 3145744 | tf_op jit(solution)/shard_map/all_gather | solution.py:199
  403.7 34.7 %all-reduce.26.cloned.1.call-done = (bf16[128,1536]{1,0:T(8,128)(2,1)}, bf16[128,1536]{1,0:T(8,128)(2,1)}) async-done(((bf16[128,1536]{1,0:T(8,128)(2,1)}, bf16[128,1536]{1,0:T(8,128)(2,1)}), (bf16[128,1536]{1,0:T(8,128)(2,1)}, bf16[128,1536]{1,0:T(8,128)(2,1)})) %all-reduce.26.cloned.1.call-update) | async-done | bytes 786448 | tf_op jit(solution)/shard_map/psum | solution.py:336
  456.9 12.0 fusion.34
  468.9 12.3 %fusion.45 = f32[1536,6,64]{0,2,1:T(8,128)} fusion(bf16[128,6,64]{0,2,1:T(8,128)(2,1)} %bitcast.401, f32[6,128,1536]{2,1,0:T(8,128)} %fusion.236, f32[6,128,1536]{2,1,0:T(8,128)} %copy-done.8, f32[6,128]{1,0:T(8,128)} %log_add_fusion.2), kind=kOutput, calls=%fused_computation.55 | convolution fusion | flops 159254784 | bytes 11897856 | tf_op jit(solution)/shard_map/hts,thd->shd/dot_general | solution.py:106
  492.4 12.0 fusion.40
  538.2 15.7 %multiply_reduce_fusion.2 = (f32[6,64]{1,0:T(8,128)}, f32[1536,6]{0,1:T(8,128)}, f32[1536,6]{0,1:T(8,128)}, f32[6,64]{1,0:T(8,128)}, f32[1536,6,64]{0,2,1:T(8,128)}) fusion(f32[1536,6,64]{0,2,1:T(8,128)} %get-tuple-element.256, f32[1536,6]{0,1:T(8,128)} %copy-done.108, f32[6,64]{1,0:T(8,128)S(1)} %copy-done.134, f32[1536,6,64]{0,2,1:T(8,128)} %get-tuple-element.262, ...), kind=kOutput, calls=%fused_computation.76 | convolution fusion | flops 166313472 | bytes 19127808 | tf_op jit(solution)/shard_map/hts,thd->shd/dot_general | solution.py:106
  569.0 8.4 fusion.282
  577.5 12.2 add_bitcast_fusion.1
  597.2 8.5 fusion.283
  670.1 26.9 %all-reduce.15 = (f32[1536]{0:T(1024)S(1)}, f32[1536]{0:T(1024)S(1)}, f32[64,6]{1,0:T(8,128)S(1)}, f32[64,6]{1,0:T(8,128)S(1)}, f32[64,6]{1,0:T(8,128)S(1)}, /*index=5*/f32[6]{0:T(128)}) all-reduce(f32[1536]{0:T(1024)S(1)} %add.540, f32[1536]{0:T(1024)S(1)} %add.541, ...), channel_id=27, replica_groups=mesh['dp'=8,'tensor'=4] {'dp'}, use_global_device_ids=true, to_apply=%region_71.72.clone | all-reduce | flops 4230 | bytes 33840
  706.7 63.0 %reduce-scatter.21.cloned.1.call-done = f32[512,384]{0,1:T(8,128)} async-done(((f32[4096,384]{0,1:T(8,128)}), f32[512,384]{0,1:T(8,128)}) %reduce-scatter.21.cloned.1.call-update) | async-done | bytes 786448 | tf_op jit(solution)/shard_map/reduce_scatter | solution.py:120
  772.0 44.0 %reduce-scatter.11.cloned.1.call-done = f32[192,384]{1,0:T(8,128)} async-done(((f32[1536,384]{1,0:T(8,128)}), f32[192,384]{1,0:T(8,128)}) %reduce-scatter.11.cloned.1.call-update) | async-done | bytes 294928 | tf_op jit(solution)/shard_map/reduce_scatter | solution.py:115
  816.0 46.6 %reduce-scatter.13.cloned.1.call-done = f32[192,384]{1,0:T(8,128)} async-done(((f32[1536,384]{1,0:T(8,128)}), f32[192,384]{1,0:T(8,128)}) %reduce-scatter.13.cloned.1.call-update) | async-done | bytes 294928 | tf_op jit(solution)/shard_map/reduce_scatter | solution.py:116
  862.7 46.3 %reduce-scatter.15.cloned.1.call-done = f32[192,384]{1,0:T(8,128)} async-done(((f32[1536,384]{1,0:T(8,128)}), f32[192,384]{1,0:T(8,128)}) %reduce-scatter.15.cloned.1.call-update) | async-done | bytes 294928 | tf_op jit(solution)/shard_map/reduce_scatter | solution.py:117
  909.0 46.8 %reduce-scatter.17.cloned.1.call-done = f32[192,384]{1,0:T(8,128)} async-done(((f32[1536,384]{1,0:T(8,128)}), f32[192,384]{1,0:T(8,128)}) %reduce-scatter.17.cloned.1.call-update) | async-done | bytes 294928 | tf_op jit(solution)/shard_map/reduce_scatter | solution.py:118
  955.8 65.6 %reduce-scatter.23.cloned.1.call-done = f32[192,1024]{1,0:T(8,128)} async-done(((f32[1536,1024]{1,0:T(8,128)}), f32[192,1024]{1,0:T(8,128)}) %reduce-scatter.23.cloned.1.call-update) | async-done | bytes 786448 | tf_op jit(solution)/shard_map/reduce_scatter | solution.py:121
  1021.3 66.1 %reduce-scatter.25.cloned.1.call-done = f32[192,1024]{1,0:T(8,128)} async-done(((f32[1536,1024]{1,0:T(8,128)}), f32[192,1024]{1,0:T(8,128)}) %reduce-scatter.25.cloned.1.call-update) | async-done | bytes 786448 | tf_op jit(solution)/shard_map/reduce_scatter | solution.py:122
  1087.4 65.7 %reduce-scatter.27.cloned.1.call-done = f32[192,1024]{1,0:T(8,128)} async-done(((f32[1536,1024]{1,0:T(8,128)}), f32[192,1024]{1,0:T(8,128)}) %reduce-scatter.27.cloned.1.call-update) | async-done | bytes 786448 | tf_op jit(solution)/shard_map/reduce_scatter | solution.py:123
  1153.2 66.1 %reduce-scatter.29.cloned.1.call-done = f32[128,1536]{1,0:T(8,128)} async-done(((f32[1024,1536]{1,0:T(8,128)}), f32[128,1536]{1,0:T(8,128)}) %reduce-scatter.29.cloned.1.call-update) | async-done | bytes 786448 | tf_op jit(solution)/shard_map/reduce_scatter | solution.py:124
  (705 shorter events, 313.6 us)
Async XLA Ops:
  7.2 78.6 %all-gather.11.cloned.1.call-start = ((), (), s32[]{:S(2)}) async-start(), calls=%async_computation.10 | async-start | bytes 3538944 | tf_op jit(solution)/shard_map/all_gather | solution.py:200
  7.9 111.9 %all-gather.13.cloned.1.call-start = ((), (), s32[]{:S(2)}) async-start(), calls=%async_computation.11 | async-start | bytes 1327104 | tf_op jit(solution)/shard_map/all_gather | solution.py:193
  8.7 115.2 %all-gather.17.cloned.1.call-start = ((), (), s32[]{:S(2)}) async-start(), calls=%async_computation.13 | async-start | bytes 1327104 | tf_op jit(solution)/shard_map/all_gather | solution.py:192
  9.4 127.1 %all-gather.15.cloned.1.call-start = ((), (), s32[]{:S(2)}) async-start(), calls=%async_computation.12 | async-start | bytes 1327104 | tf_op jit(solution)/shard_map/all_gather | solution.py:191
  10.0 145.6 %all-gather.21.cloned.1.call-start = ((), (), s32[]{:S(2)}) async-start(), calls=%async_computation.15 | async-start | bytes 3538944 | tf_op jit(solution)/shard_map/all_gather | solution.py:195
  10.6 191.9 %all-gather.19.cloned.1.call-start = ((), (), s32[]{:S(2)}) async-start(), calls=%async_computation.14 | async-start | bytes 3538944 | tf_op jit(solution)/shard_map/all_gather | solution.py:196
  11.1 218.6 %all-gather.23.cloned.1.call-start = ((), (), s32[]{:S(2)}) async-start(), calls=%async_computation.16 | async-start | bytes 1327104 | tf_op jit(solution)/shard_map/all_gather | solution.py:194
  11.9 266.9 %all-reduce.28.cloned.1.call-start = ((), (), s32[]{:S(2)}) async-start(), calls=%async_computation.32 | async-start | bytes 1572864 | tf_op jit(solution)/shard_map/psum | solution.py:282
  12.8 72.9 %copy-start.125 = (bf16[1,6,1024]{2,0,1:T(2,128)(2,1)}, bf16[1,6,1024]{2,0,1:T(2,128)(2,1)S(1)}, u32[]{:S(2)}) copy-start(bf16[1,6,1024]{2,0,1:T(2,128)(2,1)S(1)} %get-tuple-element.206) | copy-start | bytes 36868
  12.9 89.6 %copy-start.123 = (bf16[1,6,1024]{2,0,1:T(2,128)(2,1)}, bf16[1,6,1024]{2,0,1:T(2,128)(2,1)S(1)}, u32[]{:S(2)}) copy-start(bf16[1,6,1024]{2,0,1:T(2,128)(2,1)S(1)} %get-tuple-element.207) | copy-start | bytes 36868
  13.8 88.0 %copy-start.190 = (s32[6,1]{0,1:T(1,128)}, s32[6,1]{0,1:T(1,128)S(1)}, u32[]{:S(2)}) copy-start(s32[6,1]{0,1:T(1,128)S(1)} %reduce-window.14) | copy-start | bytes 76
  13.9 102.5 %copy-start.188 = (s32[6,1]{0,1:T(1,128)}, s32[6,1]{0,1:T(1,128)S(1)}, u32[]{:S(2)}) copy-start(s32[6,1]{0,1:T(1,128)S(1)} %reduce-window.15) | copy-start | bytes 76
  53.9 62.6 %copy-start.192 = (s32[6]{0:T(128)}, s32[6]{0:T(128)S(1)}, u32[]{:S(2)}) copy-start(s32[6]{0:T(128)S(1)} %get-tuple-element.268) | copy-start | bytes 76
  102.5 178.9 %copy-start.2 = (f32[128,6144]{1,0:T(8,128)}, f32[128,6144]{1,0:T(8,128)S(1)}, u32[]{:S(2)}) copy-start(f32[128,6144]{1,0:T(8,128)S(1)} %fusion.242) | copy-start | bytes 9437188
  234.9 77.6 %all-gather.25.cloned.1.call-start = ((), (), s32[]{:S(2)}) async-start(), calls=%async_computation.17 | async-start | bytes 3538944 | tf_op jit(solution)/shard_map/all_gather | solution.py:197
  235.6 111.0 %all-gather.27.cloned.1.call-start = ((), (), s32[]{:S(2)}) async-start(), calls=%async_computation.18 | async-start | bytes 3538944 | tf_op jit(solution)/shard_map/all_gather | solution.py:198
  236.2 144.6 %all-gather.29.cloned.1.call-start = ((), (), s32[]{:S(2)}) async-start(), calls=%async_computation.19 | async-start | bytes 3538944 | tf_op jit(solution)/shard_map/all_gather | solution.py:199
  237.0 201.5 %all-reduce.26.cloned.1.call-start = ((), (), s32[]{:S(2)}) async-start(), calls=%async_computation.31 | async-start | bytes 1572864 | tf_op jit(solution)/shard_map/psum | solution.py:336
  284.1 69.3 %copy-start.23 = (bf16[128,1536]{1,0:T(8,128)(2,1)}, bf16[128,1536]{1,0:T(8,128)(2,1)S(1)}, u32[]{:S(2)}) copy-start(bf16[128,1536]{1,0:T(8,128)(2,1)S(1)} %get-tuple-element.223) | copy-start | bytes 1179652
  394.6 255.2 %all-reduce.24.cloned.1.call-start = ((), (), s32[]{:S(2)}) async-start(), calls=%async_computation.30 | async-start | bytes 3145728 | tf_op jit(solution)/shard_map/psum | solution.py:292
  447.5 142.3 %copy-start.34 = (f32[128,384]{0,1:T(8,128)}, f32[128,384]{0,1:T(8,128)S(1)}, u32[]{:S(2)}) copy-start(f32[128,384]{0,1:T(8,128)S(1)} %fusion.273) | copy-start | bytes 589828
  452.8 140.9 %copy-start.36 = (f32[128,384]{0,1:T(8,128)}, f32[128,384]{0,1:T(8,128)S(1)}, u32[]{:S(2)}) copy-start(f32[128,384]{0,1:T(8,128)S(1)} %fusion.276) | copy-start | bytes 589828
  569.0 135.5 %reduce-scatter.19.cloned.1.call-start = ((), (), s32[]{:S(2)}) async-start(), calls=%async_computation.24 | async-start | bytes 7077888 | tf_op jit(solution)/shard_map/reduce_scatter | solution.py:119
  589.7 180.1 %reduce-scatter.21.cloned.1.call-start = ((), (), s32[]{:S(2)}) async-start(), calls=%async_computation.25 | async-start | bytes 7077888 | tf_op jit(solution)/shard_map/reduce_scatter | solution.py:120
  612.6 203.4 %reduce-scatter.11.cloned.1.call-start = ((), (), s32[]{:S(2)}) async-start(), calls=%async_computation.20 | async-start | bytes 2654208 | tf_op jit(solution)/shard_map/reduce_scatter | solution.py:115
  617.1 245.6 %reduce-scatter.13.cloned.1.call-start = ((), (), s32[]{:S(2)}) async-start(), calls=%async_computation.21 | async-start | bytes 2654208 | tf_op jit(solution)/shard_map/reduce_scatter | solution.py:116
  621.5 287.5 %reduce-scatter.15.cloned.1.call-start = ((), (), s32[]{:S(2)}) async-start(), calls=%async_computation.22 | async-start | bytes 2654208 | tf_op jit(solution)/shard_map/reduce_scatter | solution.py:117
  626.3 329.5 %reduce-scatter.17.cloned.1.call-start = ((), (), s32[]{:S(2)}) async-start(), calls=%async_computation.23 | async-start | bytes 2654208 | tf_op jit(solution)/shard_map/reduce_scatter | solution.py:118
  630.9 390.5 %reduce-scatter.23.cloned.1.call-start = ((), (), s32[]{:S(2)}) async-start(), calls=%async_computation.26 | async-start | bytes 7077888 | tf_op jit(solution)/shard_map/reduce_scatter | solution.py:121
  636.7 450.7 %reduce-scatter.25.cloned.1.call-start = ((), (), s32[]{:S(2)}) async-start(), calls=%async_computation.27 | async-start | bytes 7077888 | tf_op jit(solution)/shard_map/reduce_scatter | solution.py:122
  642.4 510.8 %reduce-scatter.27.cloned.1.call-start = ((), (), s32[]{:S(2)}) async-start(), calls=%async_computation.28 | async-start | bytes 7077888 | tf_op jit(solution)/shard_map/reduce_scatter | solution.py:123
  649.5 569.8 %reduce-scatter.29.cloned.1.call-start = ((), (), s32[]{:S(2)}) async-start(), calls=%async_computation.29 | async-start | bytes 7077888 | tf_op jit(solution)/shard_map/reduce_scatter | solution.py:124
  (206 other events, 1521.2 us)
Sparse Core Ops, SparseCore 0:
  9.9 33.7 all-gather.10
  45.5 24.0 all-gather.12
  71.5 24.0 all-gather.16
  97.4 24.0 all-gather.14
  123.2 32.3 all-gather.20
  157.3 32.3 all-gather.18
  191.6 24.0 all-gather.22
  235.0 43.6 all-reduce.27
  280.7 31.8 all-gather.24
  314.3 32.3 all-gather.26
  348.5 32.3 all-gather.28
  394.7 43.6 all-reduce.25
  569.1 68.8 all-reduce.23
  641.2 63.1 reduce-scatter.18
  708.0 61.6 reduce-scatter.20
  773.5 42.4 reduce-scatter.10
  820.2 42.4 reduce-scatter.12
  866.5 42.4 reduce-scatter.14
  913.3 42.4 reduce-scatter.16
  959.6 61.7 reduce-scatter.22
  1025.7 61.7 reduce-scatter.24
  1091.4 61.7 reduce-scatter.26
  1157.5 61.7 reduce-scatter.28
where the time goes:
time: 1240 us; the launch traced here: 1230 us
  waiting for transfers between devices  682 us (55%)
  matrix products  273 us (22%)
  blocking collectives  93.4 us (8%)
  local copies, waits for them, and re-layouts  82.3 us (7%)
  other arithmetic  74.2 us (6%)
  between operations  19.1 us (2%)
    dot_general x20, matrix products, contract_rows(): lax.dot_general(left, right, (((0,), (0,)), ((), ())), preferred_element_...  76.7 us
    reduce_scatter x1, waiting for transfers between devices, share_each(): lax.psum_scatter(grads[9], 'dp', scatter_dimension=0, tiled=True)  66.1 us
    reduce_scatter x1, waiting for transfers between devices, share_each(): lax.psum_scatter(grads[7], 'dp', scatter_dimension=0, tiled=True)  66.1 us
    reduce_scatter x1, waiting for transfers between devices, share_each(): lax.psum_scatter(grads[8], 'dp', scatter_dimension=0, tiled=True)  65.7 us
    reduce_scatter x1, waiting for transfers between devices, share_each(): lax.psum_scatter(grads[6], 'dp', scatter_dimension=0, tiled=True)  65.6 us
    reduce_scatter x1, waiting for transfers between devices, share_each(): lax.psum_scatter(grads[5], 'dp', scatter_dimension=0, tiled=True)  63 us
    reduce_scatter x1, waiting for transfers between devices, share_each(): lax.psum_scatter(grads[3], 'dp', scatter_dimension=0, tiled=True)  46.8 us
    reduce_scatter x1, waiting for transfers between devices, share_each(): lax.psum_scatter(grads[1], 'dp', scatter_dimension=0, tiled=True)  46.6 us
  transfers between devices with their start and end apart: 23, of which 16 were waited for; matrix products, arithmetic and copies ran while one was open for 22% of the time, Pallas kernels for 0%

commit v1 on v0

v1 whole, which is shorter than its diff:
```python
import functools

import jax
import jax.numpy as jnp
from jax import lax
from jax.sharding import PartitionSpec as P

HEAD_DIM = 64
DT = 4096
TXT = 256


EPSILON = 1e-06
MASKED = -1e30
ROPE_BASE = 10000.0


def image_layout(shapes, count):
    height = shapes[:, 0]
    stride_all = shapes[:, 1] + 1
    extent = height * stride_all
    finish = jnp.cumsum(extent)
    begin = finish - extent
    places = jnp.arange(count, dtype=jnp.int32)
    member = (places[:, None] >= begin[None, :]) & (places[:, None] < finish[None, :])
    member_int = member.astype(jnp.int32)
    inside = jnp.sum(member_int, axis=1)
    slot_ids = jnp.arange(shapes.shape[0], dtype=jnp.int32)
    segment = jnp.sum(member_int * slot_ids[None, :], axis=1)
    stride = jnp.sum(member_int * stride_all[None, :], axis=1) + 1 - inside
    offset = places - jnp.sum(member_int * begin[None, :], axis=1)
    return (member.astype(jnp.float32), segment, inside, offset // stride, offset % stride)


def rope_tables(row_pos, col_pos):
    quarter = HEAD_DIM // 4
    freq = ROPE_BASE ** (-jnp.arange(quarter, dtype=jnp.float32) / quarter)
    angles = jnp.stack(
        [
            row_pos.astype(jnp.float32)[:, None] * freq[None, :],
            col_pos.astype(jnp.float32)[:, None] * freq[None, :],
        ],
        axis=1,
    )
    return (jnp.cos(angles), jnp.sin(angles))


def rotate(values, cosine_table, sine_table):
    count, heads, width = values.shape
    parts = values.reshape(count, heads, 2, 2, width // 4)
    former = parts[:, :, :, 0, :]
    latter = parts[:, :, :, 1, :]
    cos_wide = cosine_table[:, None, :, :]
    sin_wide = sine_table[:, None, :, :]
    turned = jnp.stack(
        [former * cos_wide - latter * sin_wide, latter * cos_wide + former * sin_wide], axis=3
    )
    return turned.reshape(count, heads, width)


def head_norm(values, gain):
    scale = lax.rsqrt(jnp.mean(values * values, axis=-1, keepdims=True) + EPSILON)
    return values * scale * gain.T[None, :, :]


def modulate(values, gain, scale):
    normed = values * lax.rsqrt(jnp.mean(values * values, axis=1, keepdims=True) + EPSILON)
    return normed * gain * (1.0 + scale)


def activate(gate_val, up_val):
    return jax.nn.silu(gate_val) * up_val


def contract_rows(left, right):
    return lax.dot_general(
        left, right, (((0,), (0,)), ((), ())), preferred_element_type=jnp.float32
    )


def contract_cols(left, right):
    return lax.dot_general(
        left, right, (((1,), (1,)), ((), ())), preferred_element_type=jnp.float32
    )


def score_block(queries, keys, allowed, scale):
    scores = jnp.einsum("thd,shd->hts", queries, keys, preferred_element_type=jnp.float32) * scale
    return jnp.where(allowed[None], scores, MASKED)


def attend_forward(queries, keys, values, allowed, scale):
    scores = score_block(queries, keys, allowed, scale)
    peak = jnp.max(scores, axis=2, keepdims=True)
    expo = jnp.exp(scores - peak)
    total = jnp.sum(expo, axis=2, keepdims=True)
    probs = (expo / total).astype(jnp.bfloat16)
    output = jnp.einsum("hts,shd->thd", probs, values, preferred_element_type=jnp.float32)
    return (output, peak + jnp.log(total))


def attend_backward(queries, keys, values, allowed, scale, log_total, grad_out):
    probs = jnp.exp(score_block(queries, keys, allowed, scale) - log_total)
    grad_probs = jnp.einsum("thd,shd->hts", grad_out, values, preferred_element_type=jnp.float32)
    grad_scores = probs * (grad_probs - jnp.sum(probs * grad_probs, axis=2, keepdims=True))
    scaled = (grad_scores * scale).astype(jnp.bfloat16)
    grad_query = jnp.einsum("hts,shd->thd", scaled, keys, preferred_element_type=jnp.float32)
    grad_key = jnp.einsum("hts,thd->shd", scaled, queries, preferred_element_type=jnp.float32)
    grad_value = jnp.einsum(
        "hts,thd->shd", probs.astype(jnp.bfloat16), grad_out, preferred_element_type=jnp.float32
    )
    return (grad_query, grad_key, grad_value)


def shards(
    n_dp,
    n_tensor,
    tokens,
    context,
    captions,
    shapes,
    text_len,
    w_query,
    w_key,
    w_value,
    w_out,
    w_text_key,
    w_text_value,
    w_gate,
    w_up,
    w_down,
    w_adaln,
    gain_attn,
    gain_ffn,
    gain_query,
    gain_key,
    gain_text,
    cross_gate,
    cotangent,
):
    parts = 8 if n_dp == 8 else 1
    micro, count, width = tokens.shape
    slots = shapes.shape[1]
    rows = micro * count
    images = micro * slots
    heads = w_query.shape[1] // HEAD_DIM
    local_width = heads * HEAD_DIM
    hidden_units = w_gate.shape[1]
    scale = HEAD_DIM ** (-0.5)
    dp_rank = lax.axis_index("dp")
    tensor_rank = lax.axis_index("tensor")
    order = dp_rank ^ jnp.arange(parts, dtype=jnp.int32) if parts > 1 else None

    def hop(value, mask):
        return lax.ppermute(value, "dp", [(i, i ^ mask) for i in range(n_dp)])

    def spread(shard, path):
        if parts == 1:
            return [lax.all_gather(shard, "dp", axis=0, tiled=True)]
        along_x = hop(shard, 2)
        along_y = hop(shard, 4)
        diagonal = hop(along_y, 2) if path == 0 else hop(along_x, 4)
        even = [shard, along_x, along_y, diagonal]
        odd = [hop(piece, 1) for piece in even]
        return [piece for pair in zip(even, odd) for piece in pair]

    def collect(even, odd, path):
        if parts == 1:
            return lax.psum_scatter(even[0].astype(jnp.float32), "dp", scatter_dimension=0, tiled=True)
        got = hop(odd, 1)
        pair = [even[i].astype(jnp.float32) + got[i].astype(jnp.float32) for i in range(4)]
        near, far, first, second = (1, 2, 2, 4) if path == 0 else (2, 1, 4, 2)
        got = hop(jnp.stack([pair[near], pair[3]]).astype(jnp.bfloat16), first)
        kept = pair[0] + got[0].astype(jnp.float32)
        passed = (pair[far] + got[1].astype(jnp.float32)).astype(jnp.bfloat16)
        return kept + hop(passed, second).astype(jnp.float32)

    def relative(value, axis):
        if parts == 1:
            return value
        shape = value.shape
        cut = shape[:axis] + (parts, shape[axis] // parts) + shape[axis + 1 :]
        return jnp.take(value.reshape(cut), order, axis=axis).reshape(shape)

    def tensor_shift(value, shift):
        return lax.ppermute(
            value, "tensor", [(i, (i + shift) % n_tensor) for i in range(n_tensor)]
        )

    def tensor_sum(partial):
        part_rows = partial.shape[0] // n_tensor
        partial = partial.astype(jnp.bfloat16)

        def block(rank):
            return lax.dynamic_slice_in_dim(partial, rank * part_rows, part_rows, 0)

        total = block(tensor_rank).astype(jnp.float32)
        for shift in range(1, n_tensor):
            got = tensor_shift(block((tensor_rank + shift) % n_tensor), shift)
            total = total + got.astype(jnp.float32)
        return tensor_gather(total.astype(jnp.bfloat16), 0)

    def tensor_gather(value, axis):
        got = [value] + [tensor_shift(value, shift) for shift in range(1, n_tensor)]
        stacked = jnp.stack(got)
        ranks = (tensor_rank - jnp.arange(n_tensor, dtype=jnp.int32)) % n_tensor
        placed = jnp.take(stacked, ranks, axis=0)
        return jnp.concatenate([placed[i] for i in range(n_tensor)], axis=axis)

    def grad_pieces(left, right):
        blocks = left.reshape(left.shape[0], parts, -1)
        even = jnp.einsum(
            "tpk,tn->pkn", blocks[:, 0::2], right, preferred_element_type=jnp.float32
        ).astype(jnp.bfloat16)
        if parts == 1:
            return even, None
        odd = jnp.einsum(
            "tpk,tn->pkn", blocks[:, 1::2], right, preferred_element_type=jnp.float32
        ).astype(jnp.bfloat16)
        return even, odd

    half = hidden_units // 2
    small = jnp.concatenate(
        [
            context.reshape(-1),
            gain_attn,
            gain_ffn,
            gain_query.reshape(-1),
            gain_key.reshape(-1),
            gain_text.reshape(-1),
        ]
    )
    small_all = lax.all_gather(small, "dp", axis=0)
    text_key_pieces = spread(w_text_key, 0)
    text_value_pieces = spread(w_text_value, 1)
    query_value_pieces = spread(jnp.concatenate([w_query, w_value], axis=1), 0)
    key_out_pieces = spread(jnp.concatenate([w_key, w_out], axis=1), 1)
    gate_down_pieces = spread(jnp.concatenate([w_gate, w_down[:, :half]], axis=1), 0)
    up_down_pieces = spread(jnp.concatenate([w_up, w_down[:, half:]], axis=1), 1)
    text_key_mat = relative(jnp.concatenate(text_key_pieces, axis=0), 0)
    text_value_mat = relative(jnp.concatenate(text_value_pieces, axis=0), 0)
    query_value_mat = jnp.concatenate(query_value_pieces, axis=0)
    query_mat, value_mat = query_value_mat[:, :local_width], query_value_mat[:, local_width:]
    key_out_mat = jnp.concatenate(key_out_pieces, axis=0)
    key_mat, out_mat = key_out_mat[:, :local_width], key_out_mat[:, local_width:]
    gate_down_mat = jnp.concatenate(gate_down_pieces, axis=0)
    up_down_mat = jnp.concatenate(up_down_pieces, axis=0)
    gate_mat, up_mat = gate_down_mat[:, :hidden_units], up_down_mat[:, :hidden_units]
    down_mat = jnp.concatenate(
        [gate_down_mat[:, hidden_units:], up_down_mat[:, hidden_units:]], axis=1
    )

    cuts = [context.size, gain_attn.size, gain_ffn.size] + [gain_query.size] * 3
    edges = [sum(cuts[:i]) for i in range(len(cuts) + 1)]
    context_all, attn_gain, ffn_gain, query_gain, key_gain, text_gain = [
        small_all[:, edges[i] : edges[i + 1]] for i in range(6)
    ]
    attn_gain = relative(attn_gain.reshape(width), 0)
    ffn_gain = relative(ffn_gain.reshape(width), 0)
    query_gain = query_gain.reshape(HEAD_DIM, heads)
    key_gain = key_gain.reshape(HEAD_DIM, heads)
    text_gain = text_gain.reshape(HEAD_DIM, heads)

    cond_all = context_all.reshape(n_dp * images, -1)
    cond_rows = w_adaln.shape[0]
    cond_cols = lax.dynamic_slice_in_dim(cond_all, dp_rank * cond_rows, cond_rows, 1)
    cond_act = jax.nn.silu(cond_cols.astype(jnp.float32)).astype(jnp.bfloat16)
    mod_partial = jnp.dot(cond_act, w_adaln, preferred_element_type=jnp.float32)
    mod_part = lax.psum_scatter(mod_partial, "dp", scatter_dimension=0, tiled=True)
    modulation = tensor_gather(mod_part.astype(jnp.bfloat16), 1)
    modulation = relative(modulation.reshape(images, 4, width), 2)

    layouts = [image_layout(shapes[i], count) for i in range(micro)]
    member, segment, inside, row_pos, col_pos = [
        jnp.stack([layout[j] for layout in layouts]) for j in range(5)
    ]
    tables = [rope_tables(row_pos[i], col_pos[i]) for i in range(micro)]
    cosine_table = jnp.concatenate([table[0] for table in tables])
    sine_table = jnp.concatenate([table[1] for table in tables])
    token_mod = jnp.einsum(
        "mts,mscd->cmtd",
        member.astype(jnp.bfloat16),
        modulation.reshape(micro, slots, 4, width),
        preferred_element_type=jnp.float32,
    ).reshape(4, rows, width)
    scale_attn, gate_attn, scale_ffn, gate_ffn = [token_mod[i] for i in range(4)]

    token_rel = relative(tokens.reshape(rows, width), 1)
    grad_y_rel = relative(cotangent.reshape(rows, width), 1)
    residual_in = token_rel.astype(jnp.float32)
    attn_in_f, norm_pull = jax.vjp(modulate, residual_in, attn_gain.astype(jnp.float32), scale_attn)
    attn_in = attn_in_f.astype(jnp.bfloat16)

    def prep_pos(values, gain):
        return rotate(head_norm(values, gain), cosine_table, sine_table)

    query_raw = jnp.dot(attn_in, query_mat, preferred_element_type=jnp.float32)
    query_rot_f, query_pull = jax.vjp(
        prep_pos, query_raw.reshape(rows, heads, HEAD_DIM), query_gain.astype(jnp.float32)
    )
    key_raw = jnp.dot(attn_in, key_mat, preferred_element_type=jnp.float32)
    key_rot_f, key_pull = jax.vjp(
        prep_pos, key_raw.reshape(rows, heads, HEAD_DIM), key_gain.astype(jnp.float32)
    )
    by_micro = (micro, count, heads, HEAD_DIM)
    query_rot = query_rot_f.astype(jnp.bfloat16).reshape(by_micro)
    key_rot = key_rot_f.astype(jnp.bfloat16).reshape(by_micro)
    value_proj = (
        jnp.dot(attn_in, value_mat, preferred_element_type=jnp.float32)
        .astype(jnp.bfloat16)
        .reshape(by_micro)
    )
    text_flat = captions.reshape(images * TXT, DT)
    text_raw = jnp.dot(text_flat, text_key_mat, preferred_element_type=jnp.float32)
    text_key_f, text_pull = jax.vjp(
        head_norm, text_raw.reshape(images * TXT, heads, HEAD_DIM), text_gain.astype(jnp.float32)
    )
    text_shape = (micro, slots * TXT, heads, HEAD_DIM)
    text_key = text_key_f.astype(jnp.bfloat16).reshape(text_shape)
    text_value = (
        jnp.dot(text_flat, text_value_mat, preferred_element_type=jnp.float32)
        .astype(jnp.bfloat16)
        .reshape(text_shape)
    )
    self_id = jnp.where(inside > 0, segment, slots)
    self_mask = self_id[:, :, None] == self_id[:, None, :]
    key_slot = jnp.arange(slots * TXT, dtype=jnp.int32) // TXT
    text_live = (jnp.arange(TXT, dtype=jnp.int32)[None, None, :] < text_len[:, :, None]).reshape(
        micro, slots * TXT
    )
    cross_mask = (segment[:, :, None] == key_slot[None, None, :]) & text_live[:, None, :]
    gate_tanh = jnp.tanh(cross_gate.astype(jnp.float32))[None, None, :, None]
    forward = jax.vmap(attend_forward, in_axes=(0, 0, 0, 0, None))
    backward = jax.vmap(attend_backward, in_axes=(0, 0, 0, 0, None, 0, 0))
    self_out, self_lse = forward(query_rot, key_rot, value_proj, self_mask, scale)
    cross_out, cross_lse = forward(query_rot, text_key, text_value, cross_mask, scale)
    mixed = (self_out + gate_tanh * cross_out).reshape(rows, -1).astype(jnp.bfloat16)
    attn_out = tensor_sum(contract_cols(mixed, out_mat)).astype(jnp.float32)
    hidden = residual_in + jnp.tanh(gate_attn) * attn_out
    ffn_in_f, ffn_pull = jax.vjp(modulate, hidden, ffn_gain.astype(jnp.float32), scale_ffn)
    ffn_in = ffn_in_f.astype(jnp.bfloat16)
    gate_proj = jnp.dot(ffn_in, gate_mat, preferred_element_type=jnp.float32)
    up_proj = jnp.dot(ffn_in, up_mat, preferred_element_type=jnp.float32)
    inner_f, act_pull = jax.vjp(activate, gate_proj, up_proj)
    inner = inner_f.astype(jnp.bfloat16)

    grad_y = grad_y_rel.astype(jnp.float32)
    tanh_ffn = jnp.tanh(gate_ffn)
    grad_ffn_out = (tanh_ffn * grad_y).astype(jnp.bfloat16)
    grad_inner = jnp.dot(grad_ffn_out, down_mat, preferred_element_type=jnp.float32)
    grad_gate_f, grad_up_f = act_pull(grad_inner)
    grad_gate_b = grad_gate_f.astype(jnp.bfloat16)
    grad_up_b = grad_up_f.astype(jnp.bfloat16)
    ffn_part = contract_cols(grad_gate_b, gate_mat) + contract_cols(grad_up_b, up_mat)
    grad_ffn_in = tensor_sum(ffn_part).astype(jnp.float32)
    down_0 = collect(*grad_pieces(grad_ffn_out, inner[:, :half]), 0)
    down_1 = collect(*grad_pieces(grad_ffn_out, inner[:, half:]), 1)
    grad_w_gate = collect(*grad_pieces(ffn_in, grad_gate_b), 0)
    grad_w_up = collect(*grad_pieces(ffn_in, grad_up_b), 1)
    ffn_out = tensor_sum(contract_cols(inner, down_mat)).astype(jnp.float32)
    output = (hidden + jnp.tanh(gate_ffn) * ffn_out).astype(jnp.bfloat16)
    grad_gate_ffn = grad_y * ffn_out * (1.0 - tanh_ffn * tanh_ffn)

    grad_hidden_norm, grad_ffn_gain, grad_scale_ffn = ffn_pull(grad_ffn_in)
    grad_hidden = grad_y + grad_hidden_norm
    tanh_attn = jnp.tanh(gate_attn)
    grad_attn_out = (tanh_attn * grad_hidden).astype(jnp.bfloat16)
    grad_gate_attn = grad_hidden * attn_out * (1.0 - tanh_attn * tanh_attn)
    grad_mixed = jnp.dot(grad_attn_out, out_mat, preferred_element_type=jnp.float32).reshape(
        by_micro
    )
    grad_w_out = collect(*grad_pieces(grad_attn_out, mixed), 1)
    grad_self = grad_mixed.astype(jnp.bfloat16)
    grad_cross = (gate_tanh * grad_mixed).astype(jnp.bfloat16)
    gate_total = jnp.sum(grad_mixed * cross_out, axis=(0, 1, 3)) * (
        1.0 - gate_tanh[0, 0, :, 0] * gate_tanh[0, 0, :, 0]
    )
    grad_q_self, grad_k_self, grad_v_self = backward(
        query_rot, key_rot, value_proj, self_mask, scale, self_lse, grad_self
    )
    grad_q_cross, grad_k_text, grad_v_text = backward(
        query_rot, text_key, text_value, cross_mask, scale, cross_lse, grad_cross
    )
    flat = (rows, heads, HEAD_DIM)
    grad_query_raw, grad_query_gain = query_pull((grad_q_self + grad_q_cross).reshape(flat))
    grad_key_raw, grad_key_gain = key_pull(grad_k_self.reshape(flat))
    grad_text_raw, grad_text_gain = text_pull(grad_k_text.reshape(-1, heads, HEAD_DIM))
    grad_query_b = grad_query_raw.reshape(rows, -1).astype(jnp.bfloat16)
    grad_key_b = grad_key_raw.reshape(rows, -1).astype(jnp.bfloat16)
    grad_value_b = grad_v_self.reshape(rows, -1).astype(jnp.bfloat16)
    grad_text_key_b = grad_text_raw.reshape(images * TXT, -1).astype(jnp.bfloat16)
    grad_text_value_b = grad_v_text.reshape(images * TXT, -1).astype(jnp.bfloat16)
    attn_part = (
        contract_cols(grad_query_b, query_mat)
        + contract_cols(grad_key_b, key_mat)
        + contract_cols(grad_value_b, value_mat)
    )
    grad_attn_in = tensor_sum(attn_part).astype(jnp.float32)
    grad_w_query = collect(*grad_pieces(attn_in, grad_query_b), 0)
    grad_w_key = collect(*grad_pieces(attn_in, grad_key_b), 1)
    grad_w_value = collect(*grad_pieces(attn_in, grad_value_b), 0)

    def text_pieces(right):
        full = relative(contract_rows(text_flat, right).astype(jnp.bfloat16), 0)
        blocks = full.reshape(parts, -1, full.shape[1])
        return (blocks[0::2], blocks[1::2]) if parts > 1 else (blocks, None)

    grad_w_text_key = collect(*text_pieces(grad_text_key_b), 0)
    grad_w_text_value = collect(*text_pieces(grad_text_value_b), 1)

    grad_resid_norm, grad_attn_gain, grad_scale_attn = norm_pull(grad_attn_in)
    grad_tokens = (grad_hidden + grad_resid_norm).astype(jnp.bfloat16)
    grad_token_mod = jnp.stack([grad_scale_attn, grad_gate_attn, grad_scale_ffn, grad_gate_ffn])
    grad_modulation = jnp.einsum(
        "mts,cmtd->mscd",
        member,
        grad_token_mod.reshape(4, micro, count, width),
        precision=lax.Precision.HIGHEST,
    ).reshape(images, 4, width)
    grad_modulation = relative(grad_modulation, 2).reshape(images, 4 * width)
    span = w_adaln.shape[1]
    grad_mod_part = lax.dynamic_slice_in_dim(grad_modulation, tensor_rank * span, span, 1).astype(
        jnp.bfloat16
    )
    grad_mod_all = lax.all_gather(grad_mod_part, "dp", axis=0, tiled=True)
    grad_w_adaln = contract_rows(cond_act, grad_mod_all)
    sums = jnp.concatenate(
        [
            relative(grad_attn_gain, 0),
            relative(grad_ffn_gain, 0),
            grad_query_gain.reshape(-1),
            grad_key_gain.reshape(-1),
            grad_text_gain.reshape(-1),
            gate_total,
        ]
    )
    sums = lax.psum(sums, "dp")
    head_size = HEAD_DIM * heads
    edge = 2 * width

    def own(flat_sum, shape):
        whole = flat_sum.reshape(shape)
        size = shape[0] // n_dp
        return lax.dynamic_slice_in_dim(whole, dp_rank * size, size, 0)

    head_shape = (HEAD_DIM, heads)
    return (
        relative(output, 1).reshape(micro, count, width),
        relative(grad_tokens, 1).reshape(micro, count, width),
        grad_w_query,
        grad_w_key,
        grad_w_value,
        grad_w_out,
        grad_w_text_key,
        grad_w_text_value,
        grad_w_gate,
        grad_w_up,
        jnp.concatenate([down_0, down_1], axis=1),
        grad_w_adaln,
        own(sums[:width], (width,)),
        own(sums[width:edge], (width,)),
        own(sums[edge : edge + head_size], head_shape),
        own(sums[edge + head_size : edge + 2 * head_size], head_shape),
        own(sums[edge + 2 * head_size : edge + 3 * head_size], head_shape),
        sums[edge + 3 * head_size :],
    )


def solution(mesh):
    return jax.shard_map(
        functools.partial(shards, mesh.shape["dp"], mesh.shape["tensor"]),
        mesh=mesh,
        in_specs=(
            P(None, "dp", None),
            P(None, "dp", None),
            P(None, "dp", None, None),
            P(None, "dp", None),
            P(None, "dp"),
            P("dp", "tensor"),
            P("dp", "tensor"),
            P("dp", "tensor"),
            P("dp", "tensor"),
            P("dp", "tensor"),
            P("dp", "tensor"),
            P("dp", "tensor"),
            P("dp", "tensor"),
            P("dp", "tensor"),
            P("dp", "tensor"),
            P("dp"),
            P("dp"),
            P("dp", "tensor"),
            P("dp", "tensor"),
            P("dp", "tensor"),
            P("tensor"),
            P(None, "dp", None),
        ),
        out_specs=(
            P(None, "dp", None),
            P(None, "dp", None),
            P("dp", "tensor"),
            P("dp", "tensor"),
            P("dp", "tensor"),
            P("dp", "tensor"),
            P("dp", "tensor"),
            P("dp", "tensor"),
            P("dp", "tensor"),
            P("dp", "tensor"),
            P("dp", "tensor"),
            P("dp", "tensor"),
            P("dp"),
            P("dp"),
            P("dp", "tensor"),
            P("dp", "tensor"),
            P("dp", "tensor"),
            P("tensor"),
        ),
        check_vma=False,
    )
```

time: 1240 us -> 940 us (0.76)
  waiting for transfers between devices: 682 us -> 221 us
  local copies, waits for them, and re-layouts: 82.3 us -> 261 us
  matrix products: 273 us -> 189 us
  starting transfers between devices: 1.9 us -> 85.3 us
  blocking collectives: 93.4 us -> 52.7 us
  other arithmetic: 74.2 us -> 101 us
    reduce_scatter x10 -> x0, waiting for transfers between devices: 513 us -> none  [the longest x1 66.1 us: share_each(): lax.psum_scatter(grads[9], 'dp', scatter_dimension=0, tiled=True)]
    ppermute x0 -> x99, waiting for transfers between devices: none -> 207 us  [the longest x72 115 us: hop(): return lax.ppermute(value, 'dp', [(i, i ^ mask) for i in range(n_dp)])]
    all_gather x10 -> x0, waiting for transfers between devices: 93.8 us -> none  [the longest x1 30.7 us: shards(): lax.all_gather(w_up, 'dp', axis=0, tiled=True)]
    ppermute x0 -> x99, starting transfers between devices: none -> 82.4 us  [the longest x72 49.2 us: hop(): return lax.ppermute(value, 'dp', [(i, i ^ mask) for i in range(n_dp)])]
    psum x3 -> x0, waiting for transfers between devices: 69.3 us -> none  [the longest x1 34.7 us: shards(): lax.psum(ffn_part.astype(jnp.bfloat16), 'tensor').astype(jnp.float32)]
    unnamed x442 -> x402, local copies, waits for them, and re-layouts: 24.7 us -> 75.5 us
    dot_general x20 -> x3, matrix products: 76.7 us -> 34.5 us  [contract_rows(): lax.dot_general(left, right, (((0,), (0,)), ((), ())), preferred_element_...]
    all_gather x5 -> x1, blocking collectives: 51.7 us -> 10.5 us  [shards(): grad_mod_all = lax.all_gather(grad_mod_part, 'dp', axis=0, tiled=True)]
  transfers between devices with their start and end apart: 23 -> 102, of which waited for: 16 -> 41; matrix products, arithmetic and copies ran while one was open for 22% -> 46% of each run, Pallas kernels for 0% -> 0%
where the time goes in v1:
time: 940 us; the launch traced here: 930 us
  local copies, waits for them, and re-layouts  261 us (28%)
  waiting for transfers between devices  221 us (24%)
  matrix products  189 us (20%)
  other arithmetic  101 us (11%)
  starting transfers between devices  85.3 us (9%)
  blocking collectives  52.7 us (6%)
  between operations  18.5 us (2%)
    ppermute x72, waiting for transfers between devices, hop(): return lax.ppermute(value, 'dp', [(i, i ^ mask) for i in range(n_dp)])  115 us
    ppermute x27, waiting for transfers between devices, tensor_shift(): lax.ppermute(value, 'tensor', [(i, (i + shift) % n_tensor) for i in range...  91.9 us
    unnamed x402, local copies, waits for them, and re-layouts  75.5 us
    ppermute x72, starting transfers between devices, hop(): return lax.ppermute(value, 'dp', [(i, i ^ mask) for i in range(n_dp)])  49.2 us
    dot_general x3, matrix products, contract_rows(): lax.dot_general(left, right, (((0,), (0,)), ((), ())), preferred_element_...  34.5 us
    ppermute x27, starting transfers between devices, tensor_shift(): lax.ppermute(value, 'tensor', [(i, (i + shift) % n_tensor) for i in range...  33.2 us
    gather x18, local copies, waits for them, and re-layouts, relative(): return jnp.take(value.reshape(cut), order, axis=axis).reshape(shape)  30.6 us
    dot_general x2, matrix products, attend_backward(): jnp.einsum('hts,thd->shd', scaled, queries, preferred_element_type=jnp.fl...  26.4 us
  transfers between devices with their start and end apart: 102, of which 41 were waited for; matrix products, arithmetic and copies ran while one was open for 46% of the time, Pallas kernels for 0%

profile of v1, /device:TPU:8, one launch (start us, length us, event | category | flops | bytes accessed | tf_op | source)
XLA Modules:
  0.0 929.6 jit_solution(8286393305011518243)
XLA Ops:
  58.2 14.1 %all-reduce.9.cloned.1.call-done = bf16[102528]{0:T(1024)(128)(2,1)} async-done(((bf16[102528]{0:T(1024)(128)(2,1)}), bf16[102528]{0:T(1024)(128)(2,1)}) %all-reduce.9.cloned.1.call-update) | async-done | bytes 205072
  74.1 18.3 %fusion = f32[16,1536]{1,0:T(8,128)S(1)} fusion(f32[96,1536]{1,0:T(8,128)S(1)} %fusion.231), kind=kCustom, calls=%all-reduce-scatter | all-reduce-scatter fusion | flops 196609 | bytes 688640
  166.8 8.6 collective-permute-done.45
  179.9 7.7 collective-permute-done.38
  213.2 14.9 %collective-permute-done.22 = bf16[512,384]{1,0:T(8,128)(2,1)} collective-permute-done((bf16[512,384]{1,0:T(8,128)(2,1)}, bf16[512,384]{1,0:T(8,128)(2,1)}, u32[]{:S(2)}, u32[]{:S(2)}) %collective-permute-start.22) | collective-permute-done | bytes 393248 | tf_op jit(solution)/shard_map/ppermute | solution.py:155
  274.4 6.3 broadcast_select_fusion.3
  280.6 17.1 %fusion.248 = f32[384,3072]{1,0:T(8,128)} fusion(bf16[4096,384]{1,0:T(8,128)(2,1)} %bitcast.479, bf16[3072,4096]{1,0:T(8,128)(2,1)} %bitcast.543), kind=kOutput, calls=%fused_computation.623 | convolution fusion | flops 9663676416 | bytes 33030144 | tf_op jit(solution)/shard_map/dot_general | solution.py:314
  300.7 7.4 reshape.1698
  308.1 16.8 %fusion.30 = bf16[3072,384]{0,1:T(8,128)(2,1)} fusion(bf16[4096,384]{1,0:T(8,128)(2,1)} %bitcast.478, bf16[3072,4096]{1,0:T(8,128)(2,1)} %bitcast.544), kind=kOutput, calls=%fused_computation.59 | convolution fusion | flops 9664856064 | bytes 30670848 | tf_op jit(solution)/shard_map/dot_general | solution.py:321
  324.9 6.5 reshape.1695
  331.4 5.2 fusion.244
  367.0 5.6 collective-permute-done.32
  381.6 9.6 %collective-permute-done.35 = bf16[64,1536]{1,0:T(8,128)(2,1)S(1)} collective-permute-done((bf16[64,1536]{1,0:T(8,128)(2,1)S(1)}, bf16[64,1536]{1,0:T(8,128)(2,1)S(1)}, u32[]{:S(2)}, u32[]{:S(2)}) %collective-permute-start.35) | collective-permute-done | bytes 196640 | tf_op jit(solution)/shard_map/ppermute | solution.py:186
  424.8 8.7 collective-permute-done.52
  433.5 10.5 %collective-permute-done.53 = bf16[64,1536]{1,0:T(8,128)(2,1)S(1)} collective-permute-done((bf16[64,1536]{1,0:T(8,128)(2,1)S(1)}, bf16[64,1536]{1,0:T(8,128)(2,1)S(1)}, u32[]{:S(2)}, u32[]{:S(2)}) %collective-permute-start.53) | collective-permute-done | bytes 196640 | tf_op jit(solution)/shard_map/ppermute | solution.py:186
  446.2 12.5 %collective-permute-done.58 = bf16[64,1536]{1,0:T(8,128)(2,1)S(1)} collective-permute-done((bf16[64,1536]{1,0:T(8,128)(2,1)S(1)}, bf16[64,1536]{1,0:T(8,128)(2,1)S(1)}, u32[]{:S(2)}, u32[]{:S(2)}) %collective-permute-start.58) | collective-permute-done | bytes 196640 | tf_op jit(solution)/shard_map/ppermute | solution.py:186
  464.9 10.9 %collective-permute-done.55 = bf16[64,1536]{1,0:T(8,128)(2,1)S(1)} collective-permute-done((bf16[64,1536]{1,0:T(8,128)(2,1)S(1)}, bf16[64,1536]{1,0:T(8,128)(2,1)S(1)}, u32[]{:S(2)}, u32[]{:S(2)}) %collective-permute-start.55) | collective-permute-done | bytes 196640 | tf_op jit(solution)/shard_map/ppermute | solution.py:186
  502.5 5.6 multiply_convert_fusion.2
  519.6 18.3 %fusion.28 = f32[2,6,64,128]{3,2,1,0:T(8,128)} fusion(f32[2,6,128,1536]{3,2,1,0:T(8,128)} %fusion.49, f32[2,6,128,1536]{3,2,1,0:T(8,128)} %copy-done.2, f32[2,6,128]{2,1,0:T(8,128)S(1)} %copy-done.122, f32[2,1536,6,64]{1,0,3,2:T(2,128)} %reshape.1698, f32[6,64]{1,0:T(8,128)S(1)} %copy-done.106, f32[2,1536,6]{1,2,0:T(8,128)S(1)} %bitcast.507), kind=kOutput, calls=%fused_computation.56 | convolution fusion | flops 322046976 | bytes 24067584 | tf_op jit(solution)/shard_map/vmap(hts,shd->thd)/dot_general | solution.py:107
  537.9 24.6 %multiply_reduce_fusion.1 = (f32[6,64]{1,0:T(8,128)}, f32[2,6,64,1536]{3,2,1,0:T(8,128)}) fusion(f32[2,1536,6,64]{1,0,3,2:T(2,128)} %reshape.1698, f32[2,1536,6]{1,2,0:T(8,128)} %bitcast.506, f32[2,6,128,1536]{3,2,1,0:T(8,128)} %fusion.49, f32[2,6,128,1536]{3,2,1,0:T(8,128)} %copy-done.2, f32[2,6,128]{2,1,0:T(8,128)} %log_add_fusion, ...), kind=kOutput, calls=%fused_computation.48 | convolution fusion | flops 322046592 | bytes 28589568 | tf_op jit(solution)/shard_map/vmap(hts,thd->shd)/dot_general | solution.py:108
  577.6 7.0 fusion.34
  629.1 16.3 %fusion.16 = bf16[4096,384]{0,1:T(8,128)(2,1)} fusion(bf16[3072,384]{0,1:T(8,128)(2,1)S(1)} %fusion.18, bf16[3072,4096]{1,0:T(8,128)(2,1)} %bitcast.545), kind=kOutput, calls=%fused_computation.41 | convolution fusion | flops 9665249280 | bytes 30670848 | tf_op jit(solution)/shard_map/dot_general | solution.py:76
  659.1 15.9 %fusion.17 = bf16[4096,384]{0,1:T(8,128)(2,1)} fusion(bf16[3072,384]{0,1:T(8,128)(2,1)S(1)} %bitcast.483, bf16[3072,4096]{1,0:T(8,128)(2,1)} %bitcast.546), kind=kOutput, calls=%fused_computation.42 | convolution fusion | flops 9665249280 | bytes 30670848 | tf_op jit(solution)/shard_map/dot_general | solution.py:76
  703.6 9.5 %collective-permute-done.67 = bf16[64,1536]{1,0:T(8,128)(2,1)S(1)} collective-permute-done((bf16[64,1536]{1,0:T(8,128)(2,1)S(1)}, bf16[64,1536]{1,0:T(8,128)(2,1)S(1)}, u32[]{:S(2)}, u32[]{:S(2)}) %collective-permute-start.67) | collective-permute-done | bytes 196640 | tf_op jit(solution)/shard_map/ppermute | solution.py:186
  726.3 23.9 %psum.7 = f32[4230]{0:T(1024)S(1)} all-reduce(f32[4230]{0:T(1024)S(1)} %constant_dynamic-update-slice_fusion.57), channel_id=1, replica_groups=mesh['dp'=8,'tensor'=4] {'dp'}, use_global_device_ids=true, to_apply=%region_33.39 | all-reduce | flops 4230 | bytes 33840 | tf_op jit(solution)/shard_map/psum | solution.py:437
  756.4 5.2 fusion.63
  770.0 10.5 %all-gather.1 = bf16[8,12,1536]{2,1,0:T(8,128)(2,1)} all-gather(bf16[1,12,1536]{2,1,0:T(8,128)(2,1)S(1)} %fusion.183), channel_id=1, replica_groups=mesh['dp'=8,'tensor'=4] {'dp'}, dimensions={0}, use_global_device_ids=true | all-gather | bytes 331776 | tf_op jit(solution)/shard_map/all_gather | solution.py:425
  813.2 5.6 collective-permute-done.70
  841.5 6.6 collective-permute-done.97
  858.6 5.3 collective-permute-done.98
  876.7 15.2 %collective-permute-done.91 = bf16[2,192,1024]{2,1,0:T(8,128)(2,1)S(1)} collective-permute-done((bf16[2,192,1024]{2,1,0:T(8,128)(2,1)S(1)}, bf16[2,192,1024]{2,1,0:T(8,128)(2,1)S(1)}, u32[]{:S(2)}, u32[]{:S(2)}) %collective-permute-start.91) | collective-permute-done | bytes 786464 | tf_op jit(solution)/shard_map/ppermute | solution.py:155
  895.5 13.3 %collective-permute-done.85 = bf16[2,512,384]{2,1,0:T(8,128)(2,1)S(1)} collective-permute-done((bf16[2,512,384]{2,1,0:T(8,128)(2,1)S(1)}, bf16[2,512,384]{2,1,0:T(8,128)(2,1)S(1)}, u32[]{:S(2)}, u32[]{:S(2)}) %collective-permute-start.85) | collective-permute-done | bytes 786464 | tf_op jit(solution)/shard_map/ppermute | solution.py:155
  (934 shorter events, 547.7 us)
Async XLA Ops:
  7.2 65.1 %all-reduce.9.cloned.1.call-start = ((), (), s32[]{:S(2)}) async-start(), calls=%async_computation | async-start | bytes 413696
  10.6 138.5 %collective-permute-start.10 = (bf16[192,768]{1,0:T(8,128)(2,1)}, bf16[192,768]{1,0:T(8,128)(2,1)}, u32[]{:S(2)}, u32[]{:S(2)}) collective-permute-start(bf16[192,768]{1,0:T(8,128)(2,1)} %get-tuple-element.259), channel_id=1, source_target_pairs={{0,4},{4,0},{8,12},{12,8},{16,20},{20,16},{24,28},{28,24},{1,5},{5... | collective-permute-start | bytes 884744 | tf_op jit(solution)/shard_map/ppermute | solution.py:155
  10.6 140.2 %collective-permute-start.11 = (bf16[192,768]{1,0:T(8,128)(2,1)}, bf16[192,768]{1,0:T(8,128)(2,1)}, u32[]{:S(2)}, u32[]{:S(2)}) collective-permute-start(bf16[192,768]{1,0:T(8,128)(2,1)} %get-tuple-element.259), channel_id=1, source_target_pairs={{0,8},{4,12},{8,0},{12,4},{16,24},{20,28},{24,16},{28,20},{1,9},{5... | collective-permute-start | bytes 884744 | tf_op jit(solution)/shard_map/ppermute | solution.py:155
  103.1 50.7 %collective-permute-start.3 = (bf16[192,768]{1,0:T(8,128)(2,1)}, bf16[192,768]{1,0:T(8,128)(2,1)}, u32[]{:S(2)}, u32[]{:S(2)}) collective-permute-start(bf16[192,768]{1,0:T(8,128)(2,1)} %get-tuple-element.255), channel_id=1, source_target_pairs={{0,4},{4,0},{8,12},{12,8},{16,20},{20,16},{24,28},{28,24},{1,5},{5... | collective-permute-start | bytes 884744 | tf_op jit(solution)/shard_map/ppermute | solution.py:155
  105.8 49.9 %collective-permute-start.4 = (bf16[192,768]{1,0:T(8,128)(2,1)}, bf16[192,768]{1,0:T(8,128)(2,1)}, u32[]{:S(2)}, u32[]{:S(2)}) collective-permute-start(bf16[192,768]{1,0:T(8,128)(2,1)} %get-tuple-element.255), channel_id=1, source_target_pairs={{0,8},{4,12},{8,0},{12,4},{16,24},{20,28},{24,16},{28,20},{1,9},{5... | collective-permute-start | bytes 884744 | tf_op jit(solution)/shard_map/ppermute | solution.py:155
  109.3 49.3 %collective-permute-start.18 = (bf16[512,384]{1,0:T(8,128)(2,1)}, bf16[512,384]{1,0:T(8,128)(2,1)}, u32[]{:S(2)}, u32[]{:S(2)}) collective-permute-start(bf16[512,384]{1,0:T(8,128)(2,1)} %param.42), channel_id=1, source_target_pairs={{0,8},{4,12},{8,0},{12,4},{16,24},{20,28},{24,16},{28,20},{1,9},{5... | collective-permute-start | bytes 1179656 | tf_op jit(solution)/shard_map/ppermute | solution.py:155
  157.7 30.8 %collective-permute-start.13 = (bf16[192,768]{1,0:T(8,128)(2,1)}, bf16[192,768]{1,0:T(8,128)(2,1)S(1)}, u32[]{:S(2)}, u32[]{:S(2)}) collective-permute-start(bf16[192,768]{1,0:T(8,128)(2,1)} %get-tuple-element.259), channel_id=1, source_target_pairs={{0,16},{4,20},{8,24},{12,28},{16,0},{20,4},{24,8},{28,12},{1,17},{... | collective-permute-start | bytes 884744 | tf_op jit(solution)/shard_map/ppermute | solution.py:155
  175.4 29.4 %collective-permute-start.20 = (bf16[512,384]{1,0:T(8,128)(2,1)}, bf16[512,384]{1,0:T(8,128)(2,1)S(1)}, u32[]{:S(2)}, u32[]{:S(2)}) collective-permute-start(bf16[512,384]{1,0:T(8,128)(2,1)} %param.42), channel_id=1, source_target_pairs={{0,16},{4,20},{8,24},{12,28},{16,0},{20,4},{24,8},{28,12},{1,17},{... | collective-permute-start | bytes 1179656 | tf_op jit(solution)/shard_map/ppermute | solution.py:155
  203.1 144.1 %collective-permute-start.47 = (bf16[192,1536]{1,0:T(8,128)(2,1)}, bf16[192,1536]{1,0:T(8,128)(2,1)}, u32[]{:S(2)}, u32[]{:S(2)}) collective-permute-start(bf16[192,1536]{1,0:T(8,128)(2,1)} %get-tuple-element.234), channel_id=1, source_target_pairs={{0,16},{4,20},{8,24},{12,28},{16,0},{20,4},{24,8},{28,12},{1,17},{... | collective-permute-start | bytes 1769480 | tf_op jit(solution)/shard_map/ppermute | solution.py:155
  212.1 55.2 %collective-permute-start.40 = (bf16[192,1536]{1,0:T(8,128)(2,1)}, bf16[192,1536]{1,0:T(8,128)(2,1)}, u32[]{:S(2)}, u32[]{:S(2)}) collective-permute-start(bf16[192,1536]{1,0:T(8,128)(2,1)} %get-tuple-element.232), channel_id=1, source_target_pairs={{0,16},{4,20},{8,24},{12,28},{16,0},{20,4},{24,8},{28,12},{1,17},{... | collective-permute-start | bytes 1769480 | tf_op jit(solution)/shard_map/ppermute | solution.py:155
  231.2 116.7 %collective-permute-start.46 = (bf16[192,1536]{1,0:T(8,128)(2,1)}, bf16[192,1536]{1,0:T(8,128)(2,1)}, u32[]{:S(2)}, u32[]{:S(2)}) collective-permute-start(bf16[192,1536]{1,0:T(8,128)(2,1)} %collective-permute-done.45), channel_id=1, source_target_pairs={{0,4},{4,0},{8,12},{12,8},{16,20},{20,16},{24,28},{28,24},{1,5},{5... | collective-permute-start | bytes 1769480 | tf_op jit(solution)/shard_map/ppermute | solution.py:155
  259.8 100.7 %collective-permute-start.49 = (bf16[192,1536]{1,0:T(8,128)(2,1)}, bf16[192,1536]{1,0:T(8,128)(2,1)}, u32[]{:S(2)}, u32[]{:S(2)}) collective-permute-start(bf16[192,1536]{1,0:T(8,128)(2,1)} %collective-permute-done.45), channel_id=1, source_target_pairs={{0,16},{4,20},{8,24},{12,28},{16,0},{20,4},{24,8},{28,12},{1,17},{... | collective-permute-start | bytes 1769480 | tf_op jit(solution)/shard_map/ppermute | solution.py:155
  267.4 84.4 %collective-permute-start.39 = (bf16[192,1536]{1,0:T(8,128)(2,1)S(1)}, bf16[192,1536]{1,0:T(8,128)(2,1)}, u32[]{:S(2)}, u32[]{:S(2)}) collective-permute-start(bf16[192,1536]{1,0:T(8,128)(2,1)S(1)} %copy-done.89), channel_id=1, source_target_pairs={{0,4},{4,0},{8,12},{12,8},{16,20},{20,16},{24,28},{28,24},{1,5},{5... | collective-permute-start | bytes 1769480 | tf_op jit(solution)/shard_map/ppermute | solution.py:155
  267.6 96.1 %collective-permute-start.41 = (bf16[192,1536]{1,0:T(8,128)(2,1)}, bf16[192,1536]{1,0:T(8,128)(2,1)S(1)}, u32[]{:S(2)}, u32[]{:S(2)}) collective-permute-start(bf16[192,1536]{1,0:T(8,128)(2,1)} %collective-permute-done.40), channel_id=1, source_target_pairs={{0,4},{4,0},{8,12},{12,8},{16,20},{20,16},{24,28},{28,24},{1,5},{5... | collective-permute-start | bytes 1769480 | tf_op jit(solution)/shard_map/ppermute | solution.py:155
  363.7 42.3 %collective-permute-start.50 = (bf16[192,1536]{1,0:T(8,128)(2,1)}, bf16[192,1536]{1,0:T(8,128)(2,1)}, u32[]{:S(2)}, u32[]{:S(2)}) collective-permute-start(bf16[192,1536]{1,0:T(8,128)(2,1)} %collective-permute-done.49), channel_id=1, source_target_pairs={{0,4},{4,0},{8,12},{12,8},{16,20},{20,16},{24,28},{28,24},{1,5},{5... | collective-permute-start | bytes 1769480 | tf_op jit(solution)/shard_map/ppermute | solution.py:155
  363.7 46.1 %collective-permute-start.43 = (bf16[192,1536]{1,0:T(8,128)(2,1)}, bf16[192,1536]{1,0:T(8,128)(2,1)}, u32[]{:S(2)}, u32[]{:S(2)}) collective-permute-start(bf16[192,1536]{1,0:T(8,128)(2,1)} %collective-permute-done.42), channel_id=1, source_target_pairs={{0,4},{4,0},{8,12},{12,8},{16,20},{20,16},{24,28},{28,24},{1,5},{5... | collective-permute-start | bytes 1769480 | tf_op jit(solution)/shard_map/ppermute | solution.py:155
  421.3 37.5 %collective-permute-start.58 = (bf16[64,1536]{1,0:T(8,128)(2,1)S(1)}, bf16[64,1536]{1,0:T(8,128)(2,1)S(1)}, u32[]{:S(2)}, u32[]{:S(2)}) collective-permute-start(bf16[64,1536]{1,0:T(8,128)(2,1)S(1)} %get-tuple-element.213), channel_id=1, source_target_pairs={{0,2},{1,3},{2,0},{3,1},{4,6},{5,7},{6,4},{7,5},{8,10},{9,11},{10,... | collective-permute-start | bytes 589832 | tf_op jit(solution)/shard_map/ppermute | solution.py:186
  424.7 35.0 %collective-permute-start.59 = (bf16[64,1536]{1,0:T(8,128)(2,1)S(1)}, bf16[64,1536]{1,0:T(8,128)(2,1)S(1)}, u32[]{:S(2)}, u32[]{:S(2)}) collective-permute-start(bf16[64,1536]{1,0:T(8,128)(2,1)S(1)} %get-tuple-element.212), channel_id=1, source_target_pairs={{0,3},{1,0},{2,1},{3,2},{4,7},{5,4},{6,5},{7,6},{8,11},{9,8},{10,9... | collective-permute-start | bytes 589832 | tf_op jit(solution)/shard_map/ppermute | solution.py:186
  444.2 31.7 %collective-permute-start.55 = (bf16[64,1536]{1,0:T(8,128)(2,1)S(1)}, bf16[64,1536]{1,0:T(8,128)(2,1)S(1)}, u32[]{:S(2)}, u32[]{:S(2)}) collective-permute-start(bf16[64,1536]{1,0:T(8,128)(2,1)S(1)} %add_convert_fusion.21), channel_id=1, source_target_pairs={{0,2},{1,3},{2,0},{3,1},{4,6},{5,7},{6,4},{7,5},{8,10},{9,11},{10,... | collective-permute-start | bytes 589832 | tf_op jit(solution)/shard_map/ppermute | solution.py:186
  446.2 30.3 %collective-permute-start.56 = (bf16[64,1536]{1,0:T(8,128)(2,1)S(1)}, bf16[64,1536]{1,0:T(8,128)(2,1)S(1)}, u32[]{:S(2)}, u32[]{:S(2)}) collective-permute-start(bf16[64,1536]{1,0:T(8,128)(2,1)S(1)} %add_convert_fusion.21), channel_id=1, source_target_pairs={{0,3},{1,0},{2,1},{3,2},{4,7},{5,4},{6,5},{7,6},{8,11},{9,8},{10,9... | collective-permute-start | bytes 589832 | tf_op jit(solution)/shard_map/ppermute | solution.py:186
  610.0 84.5 %collective-permute-start.63 = (bf16[64,1536]{1,0:T(8,128)(2,1)}, bf16[64,1536]{1,0:T(8,128)(2,1)}, u32[]{:S(2)}, u32[]{:S(2)}) collective-permute-start(bf16[64,1536]{1,0:T(8,128)(2,1)} %get-tuple-element.200), channel_id=1, source_target_pairs={{0,1},{1,2},{2,3},{3,0},{4,5},{5,6},{6,7},{7,4},{8,9},{9,10},{10,1... | collective-permute-start | bytes 589832 | tf_op jit(solution)/shard_map/ppermute | solution.py:186
  610.0 84.5 %collective-permute-start.64 = (bf16[64,1536]{1,0:T(8,128)(2,1)}, bf16[64,1536]{1,0:T(8,128)(2,1)}, u32[]{:S(2)}, u32[]{:S(2)}) collective-permute-start(bf16[64,1536]{1,0:T(8,128)(2,1)} %get-tuple-element.202), channel_id=1, source_target_pairs={{0,2},{1,3},{2,0},{3,1},{4,6},{5,7},{6,4},{7,5},{8,10},{9,11},{10,... | collective-permute-start | bytes 589832 | tf_op jit(solution)/shard_map/ppermute | solution.py:186
  612.1 82.5 %collective-permute-start.65 = (bf16[64,1536]{1,0:T(8,128)(2,1)}, bf16[64,1536]{1,0:T(8,128)(2,1)}, u32[]{:S(2)}, u32[]{:S(2)}) collective-permute-start(bf16[64,1536]{1,0:T(8,128)(2,1)} %get-tuple-element.201), channel_id=1, source_target_pairs={{0,3},{1,0},{2,1},{3,2},{4,7},{5,4},{6,5},{7,6},{8,11},{9,8},{10,9... | collective-permute-start | bytes 589832 | tf_op jit(solution)/shard_map/ppermute | solution.py:186
  617.3 184.2 %collective-permute-start.93 = (bf16[4,192,512]{2,1,0:T(8,128)(2,1)}, bf16[4,192,512]{2,1,0:T(8,128)(2,1)}, u32[]{:S(2)}, u32[]{:S(2)}) collective-permute-start(bf16[4,192,512]{2,1,0:T(8,128)(2,1)} %convolution_convert_fusion.11), channel_id=1, source_target_pairs={{0,4},{4,0},{8,12},{12,8},{16,20},{20,16},{24,28},{28,24},{1,5},{5... | collective-permute-start | bytes 2359304 | tf_op jit(solution)/shard_map/ppermute | solution.py:155
  617.3 186.0 %collective-permute-start.96 = (bf16[4,192,512]{2,1,0:T(8,128)(2,1)}, bf16[4,192,512]{2,1,0:T(8,128)(2,1)}, u32[]{:S(2)}, u32[]{:S(2)}) collective-permute-start(bf16[4,192,512]{2,1,0:T(8,128)(2,1)} %convolution_convert_fusion.9), channel_id=1, source_target_pairs={{0,4},{4,0},{8,12},{12,8},{16,20},{20,16},{24,28},{28,24},{1,5},{5... | collective-permute-start | bytes 2359304 | tf_op jit(solution)/shard_map/ppermute | solution.py:155
  703.6 166.2 %collective-permute-start.90 = (bf16[4,192,1024]{2,1,0:T(8,128)(2,1)}, bf16[4,192,1024]{2,1,0:T(8,128)(2,1)}, u32[]{:S(2)}, u32[]{:S(2)}) collective-permute-start(bf16[4,192,1024]{2,1,0:T(8,128)(2,1)} %convolution_convert_fusion.5), channel_id=1, source_target_pairs={{0,4},{4,0},{8,12},{12,8},{16,20},{20,16},{24,28},{28,24},{1,5},{5... | collective-permute-start | bytes 4718600 | tf_op jit(solution)/shard_map/ppermute | solution.py:155
  713.1 84.9 %collective-permute-start.75 = (bf16[4,192,384]{2,1,0:T(8,128)(2,1)}, bf16[4,192,384]{2,1,0:T(8,128)(2,1)}, u32[]{:S(2)}, u32[]{:S(2)}) collective-permute-start(bf16[4,192,384]{2,1,0:T(8,128)(2,1)} %convolution_convert_fusion.15), channel_id=1, source_target_pairs={{0,4},{4,0},{8,12},{12,8},{16,20},{20,16},{24,28},{28,24},{1,5},{5... | collective-permute-start | bytes 1769480 | tf_op jit(solution)/shard_map/ppermute | solution.py:155
  716.0 83.5 %collective-permute-start.72 = (bf16[4,192,384]{2,1,0:T(8,128)(2,1)}, bf16[4,192,384]{2,1,0:T(8,128)(2,1)}, u32[]{:S(2)}, u32[]{:S(2)}) collective-permute-start(bf16[4,192,384]{2,1,0:T(8,128)(2,1)} %convolution_convert_fusion.17), channel_id=1, source_target_pairs={{0,4},{4,0},{8,12},{12,8},{16,20},{20,16},{24,28},{28,24},{1,5},{5... | collective-permute-start | bytes 1769480 | tf_op jit(solution)/shard_map/ppermute | solution.py:155
  799.5 72.6 %collective-permute-start.87 = (bf16[4,192,1024]{2,1,0:T(8,128)(2,1)S(1)}, bf16[4,192,1024]{2,1,0:T(8,128)(2,1)S(1)}, u32[]{:S(2)}, u32[]{:S(2)}) collective-permute-start(bf16[4,192,1024]{2,1,0:T(8,128)(2,1)S(1)} %copy-done.66), channel_id=1, source_target_pairs={{0,4},{4,0},{8,12},{12,8},{16,20},{20,16},{24,28},{28,24},{1,5},{5... | collective-permute-start | bytes 4718600 | tf_op jit(solution)/shard_map/ppermute | solution.py:155
  812.2 61.8 %collective-permute-start.84 = (bf16[4,512,384]{2,1,0:T(8,128)(2,1)S(1)}, bf16[4,512,384]{2,1,0:T(8,128)(2,1)S(1)}, u32[]{:S(2)}, u32[]{:S(2)}) collective-permute-start(bf16[4,512,384]{2,1,0:T(8,128)(2,1)S(1)} %copy-done.68), channel_id=1, source_target_pairs={{0,4},{4,0},{8,12},{12,8},{16,20},{20,16},{24,28},{28,24},{1,5},{5... | collective-permute-start | bytes 4718600 | tf_op jit(solution)/shard_map/ppermute | solution.py:155
  874.2 34.5 %collective-permute-start.85 = (bf16[2,512,384]{2,1,0:T(8,128)(2,1)S(1)}, bf16[2,512,384]{2,1,0:T(8,128)(2,1)S(1)}, u32[]{:S(2)}, u32[]{:S(2)}) collective-permute-start(bf16[2,512,384]{2,1,0:T(8,128)(2,1)S(1)} %pad_maximum_fusion.9), channel_id=1, source_target_pairs={{0,16},{4,20},{8,24},{12,28},{16,0},{20,4},{24,8},{28,12},{1,17},{... | collective-permute-start | bytes 2359304 | tf_op jit(solution)/shard_map/ppermute | solution.py:155
  875.2 34.6 %collective-permute-start.82 = (bf16[2,512,384]{2,1,0:T(8,128)(2,1)S(1)}, bf16[2,512,384]{2,1,0:T(8,128)(2,1)S(1)}, u32[]{:S(2)}, u32[]{:S(2)}) collective-permute-start(bf16[2,512,384]{2,1,0:T(8,128)(2,1)S(1)} %pad_maximum_fusion.8), channel_id=1, source_target_pairs={{0,8},{4,12},{8,0},{12,4},{16,24},{20,28},{24,16},{28,20},{1,9},{5... | collective-permute-start | bytes 2359304 | tf_op jit(solution)/shard_map/ppermute | solution.py:155
  (241 other events, 3801.5 us)
Sparse Core Ops, SparseCore 0:
  20.0 52.2 all-reduce.8

commit v2 on v1

v2 whole, which is shorter than its diff:
```python
import functools

import jax
import jax.numpy as jnp
from jax import lax
from jax.experimental import pallas as pl
from jax.experimental.pallas import tpu as pltpu
from jax.sharding import PartitionSpec as P

HEAD_DIM = 64
DT = 4096
TXT = 256


EPSILON = 1e-06
MASKED = -1e30
ROPE_BASE = 10000.0
STRIP = 16
F32 = jnp.float32
BF16 = jnp.bfloat16


def image_layout(shapes, count):
    height = shapes[:, 0]
    stride_all = shapes[:, 1] + 1
    extent = height * stride_all
    finish = jnp.cumsum(extent)
    begin = finish - extent
    places = jnp.arange(count, dtype=jnp.int32)
    member = (places[:, None] >= begin[None, :]) & (places[:, None] < finish[None, :])
    member_int = member.astype(jnp.int32)
    inside = jnp.sum(member_int, axis=1)
    slot_ids = jnp.arange(shapes.shape[0], dtype=jnp.int32)
    segment = jnp.sum(member_int * slot_ids[None, :], axis=1)
    stride = jnp.sum(member_int * stride_all[None, :], axis=1) + 1 - inside
    offset = places - jnp.sum(member_int * begin[None, :], axis=1)
    return (member.astype(jnp.float32), segment, inside, offset // stride, offset % stride)


def rope_tables(row_pos, col_pos):
    quarter = HEAD_DIM // 4
    freq = ROPE_BASE ** (-jnp.arange(quarter, dtype=jnp.float32) / quarter)
    angles = jnp.stack(
        [
            row_pos.astype(jnp.float32)[:, None] * freq[None, :],
            col_pos.astype(jnp.float32)[:, None] * freq[None, :],
        ],
        axis=1,
    )
    return (jnp.cos(angles), jnp.sin(angles))


def dot_nn(left, right):
    return lax.dot_general(left, right, (((1,), (0,)), ((), ())), preferred_element_type=F32)


def dot_nt(left, right):
    return lax.dot_general(left, right, (((1,), (1,)), ((), ())), preferred_element_type=F32)


def dot_tn(left, right):
    return lax.dot_general(left, right, (((0,), (0,)), ((), ())), preferred_element_type=F32)


def struct(shape, dtype=BF16):
    return jax.ShapeDtypeStruct(shape, dtype)


def run(body, outs, ins, scratch=(), flops=0, traffic=0):
    return pl.pallas_call(
        body,
        out_shape=outs,
        in_specs=[pl.BlockSpec(memory_space=space) for _, space in ins],
        out_specs=[pl.BlockSpec(memory_space=pltpu.VMEM)] * len(outs),
        scratch_shapes=list(scratch),
        compiler_params=pltpu.CompilerParams(vmem_limit_bytes=48 * 2**20),
        cost_estimate=pl.CostEstimate(flops=flops, bytes_accessed=traffic, transcendentals=0),
    )(*[array for array, _ in ins])


def start_pieces(pieces, target, sems):
    rank = lax.axis_index("dp")
    size = pieces[0].shape[0]
    copies = []
    for index, piece in enumerate(pieces):
        owner = jnp.bitwise_xor(rank, index) if len(pieces) > 1 else 0
        place = pl.ds(pl.multiple_of(owner * size, 64), size)
        copies.append(pltpu.make_async_copy(piece, target.at[place], sems.at[index]))
    for copy in copies:
        copy.start()
    return copies


def wait_all(copies):
    for copy in copies:
        copy.wait()


def place_blocks(blocks, target, n_tensor):
    rank = lax.axis_index("tensor")
    size = blocks[0].shape[0]
    for shift, block in enumerate(blocks):
        owner = lax.rem(rank - shift + n_tensor, n_tensor)
        target[pl.ds(pl.multiple_of(owner * size, 16), size), :] = block[...]


def cut_blocks(source, outs, n_tensor):
    rank = lax.axis_index("tensor")
    size = outs[0].shape[0]
    for shift, out in enumerate(outs):
        owner = lax.rem(rank + shift, n_tensor)
        out[...] = source[pl.ds(pl.multiple_of(owner * size, 16), size), :]


def token_columns(member, mods, which, target, n_tensor):
    rank = lax.axis_index("tensor")
    chosen = mods[0][...]
    for shift in range(1, n_tensor):
        chosen = jnp.where(lax.rem(rank - shift + n_tensor, n_tensor) == which, mods[shift][...], chosen)
    target[...] = dot_nn(member[...], chosen).astype(BF16)


def over_strips(rows, step):
    @pl.loop(0, rows // STRIP)
    def _(index):
        step(pl.ds(pl.multiple_of(index * STRIP, STRIP), STRIP))


def write_pieces(left, right, even, odd, total):
    width = left.shape[1]
    step = 256
    columns = right.shape[1]
    rank = lax.axis_index("dp")
    for first in range(0, columns, step):
        span = slice(first, min(first + step, columns))
        total[:, span] = dot_tn(left[...], right[:, span]).astype(BF16)
    size = even.shape[1]
    if even.shape[0] == 1:
        even[0] = total[:, :columns]
        return
    for index in range(4):
        for out, low in ((even, 0), (odd, 1)):
            owner = jnp.bitwise_xor(rank, 2 * index + low)
            out[index] = total[pl.ds(pl.multiple_of(owner * size, 64), size), :columns]


def head_sum(values, blocks):
    high = values.astype(BF16)
    low = (values - high.astype(F32)).astype(BF16)
    return dot_nn(high, blocks) + dot_nn(low, blocks)


def head_blocks(width):
    row = lax.broadcasted_iota(jnp.int32, (width, width), 0) // HEAD_DIM
    column = lax.broadcasted_iota(jnp.int32, (width, width), 1) // HEAD_DIM
    return jnp.where(row == column, 1.0, 0.0).astype(BF16)


def swap_pairs(values):
    width = values.shape[1]
    quarter = HEAD_DIM // 4
    lane = lax.broadcasted_iota(jnp.int32, values.shape, 1)
    former = lax.rem(lane, 2 * quarter) < quarter
    return jnp.where(
        former, pltpu.roll(values, width - quarter, 1), pltpu.roll(values, quarter, 1)
    )


def head_norm(values, gain, blocks):
    scale = lax.rsqrt(head_sum(values * values, blocks) * (1.0 / HEAD_DIM) + EPSILON)
    return values * scale * gain


def head_norm_back(values, gain, grad, blocks):
    scale = lax.rsqrt(head_sum(values * values, blocks) * (1.0 / HEAD_DIM) + EPSILON)
    normed = values * scale
    grad_gain = jnp.sum(grad * normed, axis=0, keepdims=True)
    inner = grad * gain
    mean = head_sum(inner * normed, blocks) * (1.0 / HEAD_DIM)
    return scale * (inner - normed * mean), grad_gain


def row_scale(values):
    return lax.rsqrt(jnp.mean(values * values, axis=1, keepdims=True) + EPSILON)


def project_kernel(
    n_tensor, parts, tokens, member, gain, q_gain, k_gain, cosine, sine, *rest
):
    mods, rest = rest[:n_tensor], rest[n_tensor:]
    pieces_a, pieces_b, rest = rest[:parts], rest[parts : 2 * parts], rest[2 * parts :]
    attn_in, query_raw, key_raw, query_rot, key_rot, value, mat_a, mat_b, mod, sems = rest
    copies = start_pieces(pieces_a, mat_a, sems.at[0]) + start_pieces(pieces_b, mat_b, sems.at[1])
    width = q_gain.shape[1]
    token_columns(member, mods, 0, mod, n_tensor)
    blocks = head_blocks(width)

    def step(at):
        x = tokens[at, :].astype(F32)
        normed = x * row_scale(x)
        attn_in[at, :] = (normed * gain[...] * (1.0 + mod[at, :].astype(F32))).astype(BF16)

    over_strips(tokens.shape[0], step)
    wait_all(copies)
    query_raw[...] = dot_nn(attn_in[...], mat_a[:, :width])
    key_raw[...] = dot_nn(attn_in[...], mat_b[:, :width])
    value[...] = dot_nn(attn_in[...], mat_a[:, width:]).astype(BF16)
    for raw, head_gain, out in ((query_raw, q_gain, query_rot), (key_raw, k_gain, key_rot)):
        normed = head_norm(raw[...], head_gain[...], blocks)
        out[...] = (normed * cosine[...] + swap_pairs(normed) * sine[...]).astype(BF16)


def text_kernel(
    parts, live, source, captions, gain, *rest
):
    pieces_k, pieces_v, rest = rest[:parts], rest[parts : 2 * parts], rest[2 * parts :]
    text_raw, text_key, text_value, mat_k, mat_v, sems = rest
    image = pl.program_id(0)

    @pl.when(image == 0)
    def _():
        wait_all(
            start_pieces(pieces_k, mat_k, sems.at[0]) + start_pieces(pieces_v, mat_v, sems.at[1])
        )

    @pl.when(live[image] > 0)
    def _():
        raw = dot_nn(captions[0], mat_k[...])
        text_raw[0] = raw.astype(BF16)
        text_key[0] = head_norm(raw, gain[...], head_blocks(raw.shape[1])).astype(BF16)
        text_value[0] = dot_nn(captions[0], mat_v[...]).astype(BF16)


def softmax(scores, allowed, rows_live):
    scores = jnp.where(allowed, scores, MASKED)
    expo = jnp.where(allowed, jnp.exp(scores - jnp.max(scores, axis=1, keepdims=True)), 0.0)
    total = jnp.sum(expo, axis=1, keepdims=True)
    if rows_live is not None:
        total = jnp.where(rows_live, total, 1.0)
    return expo / total


def attend_kernel(
    n_tensor, parts, micro, scale, live, text_len, query, key, value, text_key, text_value,
    self_id, self_row, segment, gate, *rest
):
    pieces_b, rest = rest[:parts], rest[parts:]
    mixed, cross_out, rest = rest[0], rest[1], rest[2:]
    partials, (mat_b, whole, sems) = rest[:n_tensor], rest[n_tensor:]
    copies = start_pieces(pieces_b, mat_b, sems)
    rows, width = query.shape
    count = rows // micro
    slots = text_key.shape[0] // micro
    heads = width // HEAD_DIM
    cross_out[...] = jnp.zeros_like(cross_out)

    @pl.loop(0, micro * slots)
    def _(image):
        @pl.when(live[image] > 0)
        def _():
            at = pl.ds(pl.multiple_of((image // slots) * count, count), count)
            mine = segment[at, :] == lax.rem(image, slots)
            column = lax.broadcasted_iota(jnp.int32, (count, TXT), 1)
            allowed = mine & (column < text_len[image])
            for head in range(heads):
                lanes = slice(head * HEAD_DIM, (head + 1) * HEAD_DIM)
                scores = dot_nt(query[at, lanes], text_key[image, :, lanes]) * scale
                probs = softmax(scores, allowed, mine).astype(BF16)
                cross_out[at, lanes] += dot_nn(probs, text_value[image, :, lanes])

    for batch in range(micro):
        at = slice(batch * count, (batch + 1) * count)
        allowed = self_id[at, :] == self_row[batch : batch + 1, :]
        for head in range(heads):
            lanes = slice(head * HEAD_DIM, (head + 1) * HEAD_DIM)
            scores = dot_nt(query[at, lanes], key[at, lanes]) * scale
            probs = softmax(scores, allowed, None).astype(BF16)
            out = dot_nn(probs, value[at, lanes])
            mixed[at, lanes] = (out + gate[:, lanes] * cross_out[at, lanes]).astype(BF16)
    wait_all(copies)
    whole[...] = dot_nt(mixed[...], mat_b[:, width:]).astype(BF16)
    cut_blocks(whole, partials, n_tensor)


def feed_kernel(
    n_tensor, parts, tokens, member, gain, cotangent, *rest
):
    mods, rest = rest[:n_tensor], rest[n_tensor:]
    sums, rest = rest[:n_tensor], rest[n_tensor:]
    pieces_a, pieces_b, rest = rest[:parts], rest[parts : 2 * parts], rest[2 * parts :]
    hidden, ffn_in, inner, grad_gate, grad_up, grad_out, rest = *rest[:6], rest[6:]
    partials, rest = rest[:n_tensor], rest[n_tensor:]
    mat_a, mat_b, attn_out, mod_1, mod_2, mod_3, whole, sems = rest
    copies = start_pieces(pieces_a, mat_a, sems.at[0]) + start_pieces(pieces_b, mat_b, sems.at[1])
    place_blocks(sums, attn_out, n_tensor)
    token_columns(member, mods, 1, mod_1, n_tensor)
    token_columns(member, mods, 2, mod_2, n_tensor)
    token_columns(member, mods, 3, mod_3, n_tensor)

    def step(at):
        gate_attn = jnp.tanh(mod_1[at, :].astype(F32))
        state = tokens[at, :].astype(F32) + gate_attn * attn_out[at, :].astype(F32)
        hidden[at, :] = state
        normed = state * row_scale(state)
        ffn_in[at, :] = (normed * gain[...] * (1.0 + mod_2[at, :].astype(F32))).astype(BF16)
        gate_ffn = jnp.tanh(mod_3[at, :].astype(F32))
        grad_out[at, :] = (gate_ffn * cotangent[at, :].astype(F32)).astype(BF16)

    rows = tokens.shape[0]
    over_strips(rows, step)
    wait_all(copies)
    units = inner.shape[1]
    chunk = 256
    for first in range(0, units, chunk):
        span = slice(first, first + chunk)
        gate = dot_nn(ffn_in[...], mat_a[:, span])
        up = dot_nn(ffn_in[...], mat_b[:, span])
        half = units // 2
        down = mat_a if first < half else mat_b
        start = units + first % half
        grad_inner = dot_nn(grad_out[...], down[:, start : start + chunk])
        turn = jax.nn.sigmoid(gate)
        active = gate * turn
        inner[:, span] = (active * up).astype(BF16)
        grad_up[:, span] = (grad_inner * active).astype(BF16)
        slope = turn * (1.0 + gate * (1.0 - turn))
        grad_gate[:, span] = (grad_inner * up * slope).astype(BF16)
    width = tokens.shape[1]
    for first in range(0, width, 512):
        span = slice(first, first + 512)
        whole[:, span] = (
            dot_nt(grad_gate[...], mat_a[span, :units]) + dot_nt(grad_up[...], mat_b[span, :units])
        ).astype(BF16)
    cut_blocks(whole, partials, n_tensor)


def feed_grad_kernel(ffn_in, grad_gate, grad_up, gate_even, gate_odd, up_even, up_odd, total):
    write_pieces(ffn_in, grad_gate, gate_even, gate_odd, total)
    write_pieces(ffn_in, grad_up, up_even, up_odd, total)


def down_grad_kernel(n_tensor, parts, grad_out, inner, *rest):
    pieces_a, pieces_b, rest = rest[:parts], rest[parts : 2 * parts], rest[2 * parts :]
    even, odd, rest = rest[0], rest[1], rest[2:]
    partials, (total, mat_a, mat_b, whole, sems) = rest[:n_tensor], rest[n_tensor:]
    copies = start_pieces(pieces_a, mat_a, sems.at[0]) + start_pieces(pieces_b, mat_b, sems.at[1])
    write_pieces(grad_out, inner, even, odd, total)
    wait_all(copies)
    units = inner.shape[1]
    half = units // 2
    for first in range(0, whole.shape[1], 512):
        span = slice(first, first + 512)
        whole[:, span] = (
            dot_nt(inner[:, :half], mat_a[span, units:])
            + dot_nt(inner[:, half:], mat_b[span, units:])
        ).astype(BF16)
    cut_blocks(whole, partials, n_tensor)


def modulate_back(values, gain, shift, grad):
    scale = row_scale(values)
    normed = values * scale
    inner = grad * gain * (1.0 + shift)
    mean = jnp.mean(inner * normed, axis=1, keepdims=True)
    return scale * (inner - normed * mean), grad * normed


def mixed_grad_kernel(n_tensor, parts, hidden, member, gain, cotangent, *rest):
    mods, rest = rest[:n_tensor], rest[n_tensor:]
    sums, rest = rest[:n_tensor], rest[n_tensor:]
    pieces_b, rest = rest[:parts], rest[parts:]
    grad_hidden, grad_out, grad_mixed, mat_b, grad_in, mod_1, mod_2, sems = rest
    copies = start_pieces(pieces_b, mat_b, sems)
    place_blocks(sums, grad_in, n_tensor)
    token_columns(member, mods, 1, mod_1, n_tensor)
    token_columns(member, mods, 2, mod_2, n_tensor)

    def step(at):
        back, _ = modulate_back(
            hidden[at, :], gain[...], mod_2[at, :].astype(F32), grad_in[at, :].astype(F32)
        )
        total = cotangent[at, :].astype(F32) + back
        grad_hidden[at, :] = total
        grad_out[at, :] = (jnp.tanh(mod_1[at, :].astype(F32)) * total).astype(BF16)

    over_strips(hidden.shape[0], step)
    wait_all(copies)
    width = grad_mixed.shape[1]
    grad_mixed[...] = dot_nn(grad_out[...], mat_b[:, width:])


def attend_back_kernel(
    micro, scale, live, text_len, grad_mixed, cross_out, query, key, value, text_key, text_value,
    text_raw, query_raw, key_raw, q_gain, k_gain, t_gain, cosine, sine, self_id, self_row, segment,
    gate, grad_query_b, grad_key_b, grad_value_b, grad_text_key, grad_text_value,
    gain_sums, grad_query, grad_key, grad_cross, grad_text
):
    rows, width = query.shape
    count = rows // micro
    slots = text_key.shape[0] // micro
    heads = width // HEAD_DIM
    blocks = head_blocks(width)
    gate_sum = jnp.sum(grad_mixed[...] * cross_out[...], axis=0, keepdims=True)
    gain_sums[...] = jnp.zeros_like(gain_sums)
    gain_sums[3:4, :] = gate_sum * (1.0 - gate[...] * gate[...])
    grad_cross[...] = (gate[...] * grad_mixed[...]).astype(BF16)
    for batch in range(micro):
        at = slice(batch * count, (batch + 1) * count)
        allowed = self_id[at, :] == self_row[batch : batch + 1, :]
        for head in range(heads):
            lanes = slice(head * HEAD_DIM, (head + 1) * HEAD_DIM)
            q, k = query[at, lanes], key[at, lanes]
            grad = grad_mixed[at, lanes].astype(BF16)
            probs = softmax(dot_nt(q, k) * scale, allowed, None)
            grad_probs = dot_nt(grad, value[at, lanes])
            mean = jnp.sum(probs * grad_probs, axis=1, keepdims=True)
            scaled = (probs * (grad_probs - mean) * scale).astype(BF16)
            grad_query[at, lanes] = dot_nn(scaled, k)
            grad_key[at, lanes] = dot_tn(scaled, q)
            grad_value_b[at, lanes] = dot_tn(probs.astype(BF16), grad).astype(BF16)

    @pl.loop(0, micro * slots)
    def _(image):
        @pl.when(live[image] == 0)
        def _():
            grad_text_key[image] = jnp.zeros((TXT, width), BF16)
            grad_text_value[image] = jnp.zeros((TXT, width), BF16)

        @pl.when(live[image] > 0)
        def _():
            at = pl.ds(pl.multiple_of((image // slots) * count, count), count)
            mine = segment[at, :] == lax.rem(image, slots)
            column = lax.broadcasted_iota(jnp.int32, (count, TXT), 1)
            allowed = mine & (column < text_len[image])
            for head in range(heads):
                lanes = slice(head * HEAD_DIM, (head + 1) * HEAD_DIM)
                q, k = query[at, lanes], text_key[image, :, lanes]
                grad = grad_cross[at, lanes]
                probs = softmax(dot_nt(q, k) * scale, allowed, mine)
                grad_probs = dot_nt(grad, text_value[image, :, lanes])
                mean = jnp.sum(probs * grad_probs, axis=1, keepdims=True)
                scaled = (probs * (grad_probs - mean) * scale).astype(BF16)
                grad_query[at, lanes] += dot_nn(scaled, k)
                grad_text[:, lanes] = dot_tn(scaled, q)
                grad_text_value[image, :, lanes] = dot_tn(probs.astype(BF16), grad).astype(BF16)
            back, gain_sum = head_norm_back(
                text_raw[image].astype(F32), t_gain[...], grad_text[...], blocks
            )
            grad_text_key[image] = back.astype(BF16)
            gain_sums[2:3, :] += gain_sum

    for index, (grad, raw, gain, out) in enumerate(
        (
            (grad_query, query_raw, q_gain, grad_query_b),
            (grad_key, key_raw, k_gain, grad_key_b),
        )
    ):
        turned = grad[...] * cosine[...] + swap_pairs(grad[...] * sine[...])
        back, gain_sum = head_norm_back(raw[...], gain[...], turned, blocks)
        out[...] = back.astype(BF16)
        gain_sums[index : index + 1, :] = gain_sum


def attn_grad_kernel(
    n_tensor, parts, attn_in, grad_query, grad_key, grad_value, grad_out, mixed, *rest
):
    pieces_a, pieces_b, rest = rest[:parts], rest[parts : 2 * parts], rest[2 * parts :]
    even, odd, rest = rest[:2], rest[2:4], rest[4:]
    partials, rest = rest[:n_tensor], rest[n_tensor:]
    mat_a, mat_b, pair, whole, total, sems = rest
    copies = start_pieces(pieces_a, mat_a, sems.at[0]) + start_pieces(pieces_b, mat_b, sems.at[1])
    width = grad_query.shape[1]
    pair[:, :width] = grad_query[...]
    pair[:, width:] = grad_value[...]
    wait_all(copies)
    for first in range(0, whole.shape[1], 512):
        span = slice(first, first + 512)
        whole[:, span] = (
            dot_nt(pair[...], mat_a[span, :]) + dot_nt(grad_key[...], mat_b[span, :width])
        ).astype(BF16)
    cut_blocks(whole, partials, n_tensor)
    write_pieces(attn_in, pair, even[0], odd[0], total)
    rank = lax.axis_index("dp")
    total[:, :width] = dot_tn(attn_in[...], grad_key[...]).astype(BF16)
    total[:, width:] = dot_tn(grad_out[...], mixed[...]).astype(BF16)
    size = even[1].shape[1]
    if parts == 1:
        even[1][0] = total[...]
        return
    for index in range(4):
        for out, low in ((even[1], 0), (odd[1], 1)):
            owner = jnp.bitwise_xor(rank, 2 * index + low)
            out[index] = total[pl.ds(pl.multiple_of(owner * size, 64), size), :]


def text_grad_kernel(live, source, rank, captions, grad_key, grad_value, out_key, out_value, acc):
    image = pl.program_id(1)
    width = grad_key.shape[2]

    @pl.when(image == 0)
    def _():
        acc[...] = jnp.zeros_like(acc)

    @pl.when(live[image] > 0)
    def _():
        acc[:, :width] += dot_tn(captions[0], grad_key[image])
        acc[:, width:] += dot_tn(captions[0], grad_value[image])

    @pl.when(image == pl.num_programs(1) - 1)
    def _():
        out_key[0] = acc[:, :width].astype(BF16)
        out_value[0] = acc[:, width:].astype(BF16)


def segment_sum(member, values):
    high = values.astype(BF16)
    rest = values - high.astype(F32)
    middle = rest.astype(BF16)
    low = (rest - middle.astype(F32)).astype(BF16)
    return dot_tn(member, high) + dot_tn(member, middle) + dot_tn(member, low)


def output_kernel(n_tensor, hidden, member, gain, cotangent, *rest):
    mods, rest = rest[:n_tensor], rest[n_tensor:]
    sums, rest = rest[:n_tensor], rest[n_tensor:]
    sums_2, rest = rest[:n_tensor], rest[n_tensor:]
    result, grad_mod, grad_gain, ffn_out, grad_in, mod_2, mod_3, grad = rest
    place_blocks(sums, ffn_out, n_tensor)
    place_blocks(sums_2, grad_in, n_tensor)
    token_columns(member, mods, 2, mod_2, n_tensor)
    token_columns(member, mods, 3, mod_3, n_tensor)
    rank = lax.axis_index("tensor")
    grad_gain[...] = jnp.zeros_like(grad_gain)

    def step(at):
        state = hidden[at, :]
        gate = jnp.tanh(mod_3[at, :].astype(F32))
        out = ffn_out[at, :].astype(F32)
        result[at, :] = (state + gate * out).astype(BF16)
        up = grad_in[at, :].astype(F32)
        product = up * state * row_scale(state)
        grad_gain[...] += jnp.sum(
            product * (1.0 + mod_2[at, :].astype(F32)), axis=0, keepdims=True
        )
        grad_gate = cotangent[at, :].astype(F32) * out * (1.0 - gate * gate)
        grad[at, :] = jnp.where(rank == 2, product * gain[...], grad_gate)

    over_strips(hidden.shape[0], step)
    grad_mod[...] = segment_sum(member[...], grad[...])


def input_kernel(n_tensor, tokens, member, gain, grad_hidden, other_mod, *rest):
    mods, rest = rest[:n_tensor], rest[n_tensor:]
    sums, rest = rest[:n_tensor], rest[n_tensor:]
    sums_2, rest = rest[:n_tensor], rest[n_tensor:]
    grad_tokens, grad_mod, grad_gain, attn_out, grad_in, mod_0, mod_1, grad = rest
    place_blocks(sums, grad_in, n_tensor)
    place_blocks(sums_2, attn_out, n_tensor)
    token_columns(member, mods, 0, mod_0, n_tensor)
    token_columns(member, mods, 1, mod_1, n_tensor)
    rank = lax.axis_index("tensor")
    grad_gain[...] = jnp.zeros_like(grad_gain)

    def step(at):
        shift = mod_0[at, :].astype(F32)
        upper = grad_hidden[at, :]
        back, product = modulate_back(
            tokens[at, :].astype(F32), gain[...], shift, grad_in[at, :].astype(F32)
        )
        grad_tokens[at, :] = (upper + back).astype(BF16)
        grad_gain[...] += jnp.sum(product * (1.0 + shift), axis=0, keepdims=True)
        gate = jnp.tanh(mod_1[at, :].astype(F32))
        grad_gate = upper * attn_out[at, :].astype(F32) * (1.0 - gate * gate)
        grad[at, :] = jnp.where(rank == 0, product * gain[...], grad_gate)

    over_strips(tokens.shape[0], step)
    own = segment_sum(member[...], grad[...])
    grad_mod[...] = jnp.where(rank < 2, own, other_mod[...]).astype(BF16)


def shards(
    n_dp,
    n_tensor,
    tokens,
    context,
    captions,
    shapes,
    text_len,
    w_query,
    w_key,
    w_value,
    w_out,
    w_text_key,
    w_text_value,
    w_gate,
    w_up,
    w_down,
    w_adaln,
    gain_attn,
    gain_ffn,
    gain_query,
    gain_key,
    gain_text,
    cross_gate,
    cotangent,
):
    parts = 8 if n_dp == 8 else 1
    micro, count, width = tokens.shape
    slots = shapes.shape[1]
    rows = micro * count
    images = micro * slots
    heads = w_query.shape[1] // HEAD_DIM
    local = heads * HEAD_DIM
    units = w_gate.shape[1]
    scale = HEAD_DIM ** (-0.5)
    dp_rank = lax.axis_index("dp")
    order = dp_rank ^ jnp.arange(parts, dtype=jnp.int32) if parts > 1 else None
    vmem, smem, anywhere = pltpu.VMEM, pltpu.SMEM, pl.ANY
    dma = pltpu.SemaphoreType.DMA

    def inside(*arrays):
        return [(array, vmem) for array in arrays]

    def scalars(*arrays):
        return [(array, smem) for array in arrays]

    def outside(*arrays):
        return [(array, anywhere) for array in arrays]

    def hop(value, mask):
        return lax.ppermute(value, "dp", [(i, i ^ mask) for i in range(n_dp)])

    def spread(shard, path):
        if parts == 1:
            return [lax.all_gather(shard, "dp", axis=0, tiled=True)]
        along_x = hop(shard, 2)
        along_y = hop(shard, 4)
        diagonal = hop(along_y, 2) if path == 0 else hop(along_x, 4)
        even = [shard, along_x, along_y, diagonal]
        odd = [hop(piece, 1) for piece in even]
        return [piece for pair in zip(even, odd) for piece in pair]

    def collect(even, odd, path):
        if parts == 1:
            return lax.psum_scatter(even[0].astype(F32), "dp", scatter_dimension=0, tiled=True)
        got = hop(odd, 1)
        pair = [even[i].astype(F32) + got[i].astype(F32) for i in range(4)]
        near, far, first, second = (1, 2, 2, 4) if path == 0 else (2, 1, 4, 2)
        got = hop(jnp.stack([pair[near], pair[3]]).astype(BF16), first)
        kept = pair[0] + got[0].astype(F32)
        passed = (pair[far] + got[1].astype(F32)).astype(BF16)
        return kept + hop(passed, second).astype(F32)

    def tensor_shift(value, shift):
        return lax.ppermute(
            value, "tensor", [(i, (i + shift) % n_tensor) for i in range(n_tensor)]
        )

    def tensor_gather(value):
        return [value] + [tensor_shift(value, shift) for shift in range(1, n_tensor)]

    def tensor_sum(blocks):
        total = blocks[0].astype(F32)
        for shift in range(1, n_tensor):
            total = total + tensor_shift(blocks[shift], shift).astype(F32)
        return tensor_gather(total.astype(BF16))

    def doubled(value):
        if parts == 1:
            return lax.all_gather(value, "dp", axis=0)
        value = value[None]
        for mask in (1, 2, 4):
            value = jnp.concatenate([value, hop(value, mask)], axis=0)
        return value

    half = units // 2
    small = jnp.concatenate(
        [
            context.reshape(-1),
            gain_attn,
            gain_ffn,
            gain_query.reshape(-1),
            gain_key.reshape(-1),
            gain_text.reshape(-1),
        ]
    )
    small_all = doubled(small)
    text_key_pieces = spread(w_text_key, 0)
    text_value_pieces = spread(w_text_value, 1)
    pieces_qv = spread(jnp.concatenate([w_query, w_value], axis=1), 0)
    pieces_ko = spread(jnp.concatenate([w_key, w_out], axis=1), 1)
    pieces_gd = spread(jnp.concatenate([w_gate, w_down[:, :half]], axis=1), 0)
    pieces_ud = spread(jnp.concatenate([w_up, w_down[:, half:]], axis=1), 1)

    cuts = [context.size, gain_attn.size, gain_ffn.size] + [gain_query.size] * 3
    edges = [sum(cuts[:i]) for i in range(len(cuts) + 1)]
    context_all, *gains = [small_all[:, edges[i] : edges[i + 1]] for i in range(6)]
    if parts > 1:
        gains = [jnp.take(gain, order, axis=0) for gain in gains]
    attn_gain, ffn_gain = [gain.reshape(1, width).astype(F32) for gain in gains[:2]]
    query_gain, key_gain, text_gain = [
        gain.reshape(HEAD_DIM, heads).T.reshape(1, local).astype(F32) for gain in gains[2:]
    ]

    cond_rows = w_adaln.shape[0]
    cond_cols = lax.dynamic_slice_in_dim(
        context_all.reshape(n_dp * images, -1), dp_rank * cond_rows, cond_rows, 1
    )
    cond_act = jax.nn.silu(cond_cols.astype(F32)).astype(BF16)
    mod_partial = dot_nn(cond_act, w_adaln)
    if parts == 1:
        mod_part = lax.psum_scatter(mod_partial, "dp", scatter_dimension=0, tiled=True)
    else:
        mod_part = mod_partial.reshape(parts, images, -1)
        for mask in (4, 2, 1):
            mod_part = mod_part[:mask] + hop(mod_part[mask:], mask)
        mod_part = mod_part[0]
    mods = tensor_gather(mod_part.astype(BF16))

    layouts = [image_layout(shapes[i], count) for i in range(micro)]
    member, segment, inside_any, row_pos, col_pos = [
        jnp.stack([layout[j] for layout in layouts]) for j in range(5)
    ]
    cosine, sine = rope_tables(row_pos.reshape(rows), col_pos.reshape(rows))
    cosine = jnp.tile(jnp.stack([cosine, cosine], axis=2).reshape(rows, HEAD_DIM), (1, heads))
    sine = jnp.tile(jnp.stack([-sine, sine], axis=2).reshape(rows, HEAD_DIM), (1, heads))
    which = jnp.arange(micro, dtype=jnp.int32)
    member = jnp.where(
        (which[:, None] == which[None, :])[:, None, :, None], member[:, :, None, :], 0.0
    )
    member = member.reshape(rows, images).astype(BF16)
    self_row = jnp.where(inside_any > 0, segment, slots)
    self_id = self_row.reshape(rows, 1)
    segment = segment.reshape(rows, 1)
    lens = text_len.reshape(images)
    used = shapes[:, :, 0] * (shapes[:, :, 1] + 1) > 0
    used = used | (jnp.arange(slots)[None, :] == 0)
    live = used.reshape(images).astype(jnp.int32)
    at = jnp.arange(images, dtype=jnp.int32)
    source = lax.cummax(jnp.where(live > 0, at, 0))
    gate = jnp.repeat(jnp.tanh(cross_gate.astype(F32)), HEAD_DIM)[None, :]
    token_rows = tokens.reshape(rows, width)
    grad_y = cotangent.reshape(rows, width)
    caption_images = captions.reshape(images, TXT, DT)

    attn_in, query_raw, key_raw, query_rot, key_rot, value = run(
        functools.partial(project_kernel, n_tensor, parts),
        [struct((rows, width))]
        + [struct((rows, local), F32)] * 2
        + [struct((rows, local))] * 3,
        inside(token_rows, member, attn_gain, query_gain, key_gain, cosine, sine, *mods)
        + outside(*pieces_qv, *pieces_ko),
        [
            vmem((width, 2 * local), BF16),
            vmem((width, 2 * local), BF16),
            vmem((rows, width), BF16),
            dma((2, parts)),
        ],
        flops=6 * rows * width * local,
        traffic=10 * 2**20,
    )

    text_raw, text_key, text_value = pl.pallas_call(
        functools.partial(text_kernel, parts),
        out_shape=[struct((images, TXT, local))] * 3,
        grid_spec=pltpu.PrefetchScalarGridSpec(
            num_scalar_prefetch=2,
            grid=(images,),
            in_specs=[
                pl.BlockSpec((1, TXT, DT), lambda i, live, source: (source[i], 0, 0)),
                pl.BlockSpec((1, local), lambda i, live, source: (0, 0)),
            ]
            + [pl.BlockSpec(memory_space=anywhere)] * (2 * parts),
            out_specs=[pl.BlockSpec((1, TXT, local), lambda i, live, source: (i, 0, 0))] * 3,
            scratch_shapes=[vmem((DT, local), BF16), vmem((DT, local), BF16), dma((2, parts))],
        ),
        compiler_params=pltpu.CompilerParams(vmem_limit_bytes=40 * 2**20),
        cost_estimate=pl.CostEstimate(
            flops=2 * images * TXT * DT * local, bytes_accessed=20 * 2**20, transcendentals=0
        ),
    )(live, source, caption_images, text_gain, *text_key_pieces, *text_value_pieces)

    part_rows = rows // n_tensor
    blocks = [struct((part_rows, width))] * n_tensor
    mixed, cross_out, *attn_part = run(
        functools.partial(attend_kernel, n_tensor, parts, micro, scale),
        [struct((rows, local)), struct((rows, local), F32)] + blocks,
        scalars(live, lens)
        + inside(query_rot, key_rot, value, text_key, text_value, self_id, self_row, segment, gate)
        + outside(*pieces_ko),
        [vmem((width, 2 * local), BF16), vmem((rows, width), BF16), dma((parts,))],
        flops=2 * 2**30,
        traffic=12 * 2**20,
    )
    attn_out = tensor_sum(attn_part)

    mat = vmem((width, units + half), BF16)
    wide = vmem((rows, width), BF16)
    hidden, ffn_in, inner, grad_gate, grad_up, grad_ffn_out, *ffn_part = run(
        functools.partial(feed_kernel, n_tensor, parts),
        [struct((rows, width), F32), struct((rows, width))]
        + [struct((rows, units))] * 3
        + [struct((rows, width))]
        + blocks,
        inside(token_rows, member, ffn_gain, grad_y, *mods, *attn_out)
        + outside(*pieces_gd, *pieces_ud),
        [mat, mat, wide, wide, wide, wide, wide, dma((2, parts))],
        flops=10 * rows * width * units,
        traffic=20 * 2**20,
    )
    grad_ffn_in = tensor_sum(ffn_part)

    size = width // parts
    even_of = lambda depth, columns: struct((max(parts // 2, 1), depth, columns))
    piece = [even_of(size, units)] * 2
    down_even, down_odd, *ffn_out_part = run(
        functools.partial(down_grad_kernel, n_tensor, parts),
        piece + blocks,
        inside(grad_ffn_out, inner) + outside(*pieces_gd, *pieces_ud),
        [vmem((width, units), BF16), mat, mat, wide, dma((2, parts))],
        flops=4 * rows * width * units,
        traffic=15 * 2**20,
    )
    gate_even, gate_odd, up_even, up_odd = run(
        feed_grad_kernel,
        piece + piece,
        inside(ffn_in, grad_gate, grad_up),
        [vmem((width, units), BF16)],
        flops=4 * rows * width * units,
        traffic=8 * 2**20,
    )
    grad_down_0 = collect(down_even[:, :, :half], down_odd[:, :, :half], 0)
    grad_down_1 = collect(down_even[:, :, half:], down_odd[:, :, half:], 1)
    grad_w_gate = collect(gate_even, gate_odd, 0)
    grad_w_up = collect(up_even, up_odd, 1)

    grad_hidden, grad_attn_out, grad_mixed = run(
        functools.partial(mixed_grad_kernel, n_tensor, parts),
        [struct((rows, width), F32), struct((rows, width)), struct((rows, local), F32)],
        inside(hidden, member, ffn_gain, grad_y, *mods, *grad_ffn_in) + outside(*pieces_ko),
        [vmem((width, 2 * local), BF16), wide, wide, wide, dma((parts,))],
        flops=2 * rows * width * local,
        traffic=8 * 2**20,
    )

    tile = struct((rows, local))
    texts = struct((images, TXT, local))
    grad_query_b, grad_key_b, grad_value_b, grad_text_key, grad_text_value, gain_sums = run(
        functools.partial(attend_back_kernel, micro, scale),
        [tile, tile, tile, texts, texts, struct((8, local), F32)],
        scalars(live, lens)
        + inside(
            grad_mixed, cross_out, query_rot, key_rot, value, text_key, text_value, text_raw,
            query_raw, key_raw, query_gain, key_gain, text_gain, cosine, sine, self_id, self_row,
            segment, gate,
        ),
        [
            vmem((rows, local), F32),
            vmem((rows, local), F32),
            vmem((rows, local), BF16),
            vmem((TXT, local), F32),
        ],
        flops=4 * 2**30,
        traffic=15 * 2**20,
    )

    piece = even_of(size, 2 * local)
    qv_even, ko_even, qv_odd, ko_odd, *attn_in_part = run(
        functools.partial(attn_grad_kernel, n_tensor, parts),
        [piece] * 4 + blocks,
        inside(attn_in, grad_query_b, grad_key_b, grad_value_b, grad_attn_out, mixed)
        + outside(*pieces_qv, *pieces_ko),
        [
            vmem((width, 2 * local), BF16),
            vmem((width, 2 * local), BF16),
            vmem((rows, 2 * local), BF16),
            wide,
            vmem((width, 2 * local), BF16),
            dma((2, parts)),
        ],
        flops=14 * rows * width * local,
        traffic=15 * 2**20,
    )
    grad_attn_in = tensor_sum(attn_in_part)
    grad_qv = collect(qv_even, qv_odd, 0)
    grad_ko = collect(ko_even, ko_odd, 1)

    depth = DT // parts

    def text_grads(low):
        chosen = max(parts // 2, 1)

        def caption_place(j, i, live, source, rank):
            block = jnp.bitwise_xor(rank[0], 2 * j + low) if parts > 1 else 0
            return (source[i], 0, block)

        return pl.pallas_call(
            text_grad_kernel,
            out_shape=[even_of(depth, local)] * 2,
            grid_spec=pltpu.PrefetchScalarGridSpec(
                num_scalar_prefetch=3,
                grid=(chosen, images),
                in_specs=[
                    pl.BlockSpec((1, TXT, depth), caption_place),
                    pl.BlockSpec((images, TXT, local), lambda j, i, *_: (0, 0, 0)),
                    pl.BlockSpec((images, TXT, local), lambda j, i, *_: (0, 0, 0)),
                ],
                out_specs=[pl.BlockSpec((1, depth, local), lambda j, i, *_: (j, 0, 0))] * 2,
                scratch_shapes=[vmem((depth, 2 * local), F32)],
            ),
            compiler_params=pltpu.CompilerParams(vmem_limit_bytes=56 * 2**20),
            cost_estimate=pl.CostEstimate(
                flops=images * TXT * DT * local, bytes_accessed=10 * 2**20, transcendentals=0
            ),
        )(live, source, dp_rank[None].astype(jnp.int32), caption_images, grad_text_key, grad_text_value)

    if parts > 1:
        text_key_odd, text_value_odd = text_grads(1)
    else:
        text_key_odd, text_value_odd = None, None
    text_key_even, text_value_even = text_grads(0)
    grad_w_text_key = collect(text_key_even, text_key_odd, 0)
    grad_w_text_value = collect(text_value_even, text_value_odd, 1)

    ffn_out = tensor_sum(ffn_out_part)
    result, ffn_mod, ffn_gain_sum = run(
        functools.partial(output_kernel, n_tensor),
        [struct((rows, width)), struct((images, width), F32), struct((1, width), F32)],
        inside(hidden, member, ffn_gain, grad_y, *mods, *ffn_out, *grad_ffn_in),
        [wide, wide, wide, wide, vmem((rows, width), F32)],
        traffic=8 * 2**20,
    )
    grad_tokens, grad_mod, attn_gain_sum = run(
        functools.partial(input_kernel, n_tensor),
        [struct((rows, width)), struct((images, width)), struct((1, width), F32)],
        inside(
            token_rows, member, attn_gain, grad_hidden, ffn_mod, *mods, *grad_attn_in, *attn_out
        ),
        [wide, wide, wide, wide, vmem((rows, width), F32)],
        traffic=8 * 2**20,
    )
    grad_mod_all = doubled(grad_mod).reshape(n_dp * images, width)
    grad_w_adaln = dot_tn(cond_act, grad_mod_all)
    head_sums = gain_sums[:3].reshape(3, heads, HEAD_DIM).transpose(0, 2, 1)
    gate_sums = jnp.sum(gain_sums[3].reshape(heads, HEAD_DIM), axis=1)
    sums = jnp.concatenate(
        [attn_gain_sum[0], ffn_gain_sum[0], head_sums.reshape(-1), gate_sums]
    )
    if parts == 1:
        sums = lax.psum(sums, "dp")
    else:
        for mask in (1, 2, 4):
            sums = sums + hop(sums, mask)

    def own(first, shape):
        whole = sums[first : first + shape[0] * (shape[1] if len(shape) > 1 else 1)].reshape(shape)
        part = shape[0] // n_dp
        return lax.dynamic_slice_in_dim(whole, dp_rank * part, part, 0)

    head_shape = (HEAD_DIM, heads)
    edge = 2 * width
    return (
        result.reshape(micro, count, width),
        grad_tokens.reshape(micro, count, width),
        grad_qv[:, :local],
        grad_ko[:, :local],
        grad_qv[:, local:],
        grad_ko[:, local:],
        grad_w_text_key,
        grad_w_text_value,
        grad_w_gate,
        grad_w_up,
        jnp.concatenate([grad_down_0, grad_down_1], axis=1),
        grad_w_adaln,
        own(0, (width,)),
        own(width, (width,)),
        own(edge, head_shape),
        own(edge + local, head_shape),
        own(edge + 2 * local, head_shape),
        sums[edge + 3 * local :],
    )


def solution(mesh):
    return jax.shard_map(
        functools.partial(shards, mesh.shape["dp"], mesh.shape["tensor"]),
        mesh=mesh,
        in_specs=(
            P(None, "dp", None),
            P(None, "dp", None),
            P(None, "dp", None, None),
            P(None, "dp", None),
            P(None, "dp"),
            P("dp", "tensor"),
            P("dp", "tensor"),
            P("dp", "tensor"),
            P("dp", "tensor"),
            P("dp", "tensor"),
            P("dp", "tensor"),
            P("dp", "tensor"),
            P("dp", "tensor"),
            P("dp", "tensor"),
            P("dp", "tensor"),
            P("dp"),
            P("dp"),
            P("dp", "tensor"),
            P("dp", "tensor"),
            P("dp", "tensor"),
            P("tensor"),
            P(None, "dp", None),
        ),
        out_specs=(
            P(None, "dp", None),
            P(None, "dp", None),
            P("dp", "tensor"),
            P("dp", "tensor"),
            P("dp", "tensor"),
            P("dp", "tensor"),
            P("dp", "tensor"),
            P("dp", "tensor"),
            P("dp", "tensor"),
            P("dp", "tensor"),
            P("dp", "tensor"),
            P("dp", "tensor"),
            P("dp"),
            P("dp"),
            P("dp", "tensor"),
            P("dp", "tensor"),
            P("dp", "tensor"),
            P("tensor"),
        ),
        check_vma=False,
    )
```

time: 940 us -> 603 us (0.64)
  local copies, waits for them, and re-layouts: 261 us -> 67.5 us
  matrix products: 189 us -> 2.88 us
  Pallas kernels: 0 us -> 159 us
  other arithmetic: 101 us -> 34.4 us
  blocking collectives: 52.7 us -> 0 us
  starting transfers between devices: 85.3 us -> 124 us
  waiting for transfers between devices: 221 us -> 205 us
  between operations: 18.5 us -> 2.94 us
    dot_general x50 -> x2, matrix products: 189 us -> 2.88 us  [the longest x1 1.92 us: dot_tn(): lax.dot_general(left, right, (((0,), (0,)), ((), ())), preferred_element_...]
    pallas_call x0 -> x13, Pallas kernels: none -> 159 us  [the longest x10 95.3 us: run(): pl.pallas_call(body, out_shape=outs, in_specs=[pl.BlockSpec(memory_space=...]
    unnamed x402 -> x295, local copies, waits for them, and re-layouts: 75.5 us -> 27.1 us
    ppermute x72 -> x78, starting transfers between devices: 49.2 us -> 85.2 us  [hop(): return lax.ppermute(value, 'dp', [(i, i ^ mask) for i in range(n_dp)])]
    gather x23 -> x5, local copies, waits for them, and re-layouts: 36 us -> 4.92 us  [shards(): gains = [jnp.take(gain, order, axis=0) for gain in gains]]
    concatenate x28 -> x2, local copies, waits for them, and re-layouts: 30.3 us -> 1.87 us  [the longest x1 0.94 us: shards(): pieces_ko = spread(jnp.concatenate([w_key, w_out], axis=1), 1)]
    reshape x15 -> x6, local copies, waits for them, and re-layouts: 29.8 us -> 1.44 us  [the longest x1 0.96 us: shards(): context_all.reshape(n_dp * images, -1)]
    psum x1 -> x0, blocking collectives: 23.9 us -> none  [shards(): sums = lax.psum(sums, 'dp')]
  transfers between devices with their start and end apart: 102 -> 105, of which waited for: 41 -> 35; matrix products, arithmetic and copies ran while one was open for 46% -> 13% of each run, Pallas kernels for 0% -> 24%
where the time goes in v2:
time: 603 us; the launch traced here: 595 us
  waiting for transfers between devices  205 us (34%)
  Pallas kernels  159 us (26%)
  starting transfers between devices  124 us (21%)
  local copies, waits for them, and re-layouts  67.5 us (11%)
  other arithmetic  34.4 us (6%)
    ppermute x78, waiting for transfers between devices, hop(): return lax.ppermute(value, 'dp', [(i, i ^ mask) for i in range(n_dp)])  122 us
    pallas_call x10, Pallas kernels, run(): pl.pallas_call(body, out_shape=outs, in_specs=[pl.BlockSpec(memory_space=...  95.3 us
    ppermute x78, starting transfers between devices, hop(): return lax.ppermute(value, 'dp', [(i, i ^ mask) for i in range(n_dp)])  85.2 us
    ppermute x27, waiting for transfers between devices, tensor_shift(): lax.ppermute(value, 'tensor', [(i, (i + shift) % n_tensor) for i in range...  82.2 us
    pallas_call x2, Pallas kernels, text_grads(): pl.pallas_call(text_grad_kernel, out_shape=[even_of(depth, local)] * 2, g...  46.3 us
    ppermute x27, starting transfers between devices, tensor_shift(): lax.ppermute(value, 'tensor', [(i, (i + shift) % n_tensor) for i in range...  38.5 us
    unnamed x295, local copies, waits for them, and re-layouts  27.1 us
    pallas_call x1, Pallas kernels, shards(): pl.pallas_call(functools.partial(text_kernel, parts), out_shape=[struct((...  17.7 us
  transfers between devices with their start and end apart: 105, of which 35 were waited for; matrix products, arithmetic and copies ran while one was open for 13% of the time, Pallas kernels for 24%

profile of v2, /device:TPU:8, one launch (start us, length us, event | category | flops | bytes accessed | tf_op | source)
XLA Modules:
  0.0 595.2 jit_solution(11150115878462796925)
XLA Ops:
  17.7 3.5 collective-permute-done.1
  22.1 4.1 collective-permute-done.2
  35.3 4.7 collective-permute-done.19.rest_16_.rest_4_.rest_12_
  41.5 7.0 %collective-permute-done.3 = f32[4,12,1536]{2,1,0:T(8,128)} collective-permute-done((f32[4,12,1536]{2,1,0:T(8,128)}, f32[4,12,1536]{2,1,0:T(8,128)}, u32[]{:S(2)}, u32[]{:S(2)}) %collective-permute-start.3) | collective-permute-done | bytes 294944 | tf_op jit(solution)/shard_map/ppermute | solution.py:631
  58.7 3.9 collective-permute-done.33.rest_12_
  71.5 16.4 %collective-permute-done.21.rest_18_.rest_6_.rest_14_ = bf16[192,768]{1,0:T(8,128)(2,1)S(1)} collective-permute-done((bf16[192,768]{1,0:T(8,128)(2,1)S(1)}, bf16[192,768]{1,0:T(8,128)(2,1)S(1)}, u32[]{:S(2)}, u32[]{:S(2)}) %collective-permute-start.21) | collective-permute-done | bytes 294944 | tf_op jit(solution)/shard_map/ppermute | solution.py:631
  126.5 6.8 %shard_map.349 = (bf16[256,1536]{1,0:T(8,128)(2,1)}, f32[256,384]{1,0:T(8,128)S(1)}, f32[256,384]{1,0:T(8,128)}, bf16[256,384]{1,0:T(8,128)(2,1)S(1)}, bf16[256,...) custom-call(bf16[256,1536]{1,0:T(8,128)(2,1)} %bitcast.140, bf16[256,12]{1,0:T(8,128)(2,1)S(1)} %copy.72.member, ...), custom_call_target="tpu_custom_call" | custom-call | flops 905969664 | bytes 10485760 | tf_op jit(solution)/shard_map/pallas_call | solution.py:70
  138.4 17.7 %shard_map.350 = (bf16[12,256,384]{2,1,0:T(8,128)(2,1)S(1)}, bf16[12,256,384]{2,1,0:T(8,128)(2,1)S(1)}, bf16[12,256,384]{2,1,0:T(8,128)(2,1)S(1)}) custom-call(s32[12]{0:T(128)S(1)} %or_convert_fusion.1.live, s32[12]{0:T(128)S(1)} %bitcast.147, bf16[12,256,4096]{2,1,0:T(8,128)(2,1)} %bitcast.150, f32[1,384]{1,0:T(1,128)S(1)} %reshape.1015.gain.t_gain, ...), custom_call_target="tpu_custom_call" | custom-call | flops 9663676416 | bytes 20971520 | tf_op jit(solution)/shard_map/pallas_call | solution.py:763
  160.4 13.5 %shard_map.351 = (bf16[256,384]{1,0:T(8,128)(2,1)S(1)}, f32[256,384]{1,0:T(8,128)S(1)}, bf16[64,1536]{1,0:T(8,128)(2,1)S(1)}, bf16[64,1536]{1,0:T(8,128)(2,1)S(1...) custom-call(s32[12]{0:T(128)S(1)} %or_convert_fusion.1.live, s32[12]{0:T(128)S(1)} %reshape.1003.text_len, ...), custom_call_target="tpu_custom_call" | custom-call | flops 2147483648 | bytes 12582912 | tf_op jit(solution)/shard_map/pallas_call | solution.py:70
  178.9 9.3 %collective-permute-done.39 = bf16[64,1536]{1,0:T(8,128)(2,1)S(1)} collective-permute-done((bf16[64,1536]{1,0:T(8,128)(2,1)S(1)}, bf16[64,1536]{1,0:T(8,128)(2,1)S(1)}, u32[]{:S(2)}, u32[]{:S(2)}) %collective-permute-start.39) | collective-permute-done | bytes 196640 | tf_op jit(solution)/shard_map/ppermute | solution.py:655
  198.3 10.6 %collective-permute-done.41.rest_6_.rest_10_ = bf16[64,1536]{1,0:T(8,128)(2,1)} collective-permute-done((bf16[64,1536]{1,0:T(8,128)(2,1)S(1)}, bf16[64,1536]{1,0:T(8,128)(2,1)}, u32[]{:S(2)}, u32[]{:S(2)}) %collective-permute-start.41) | collective-permute-done | bytes 196640 | tf_op jit(solution)/shard_map/ppermute | solution.py:655
  214.8 10.1 %shard_map.352 = (f32[256,1536]{1,0:T(8,128)}, bf16[256,1536]{1,0:T(8,128)(2,1)}, bf16[256,1024]{1,0:T(8,128)(2,1)S(1)}, bf16[256,1024]{1,0:T(8,128)(2,1)S(1)}, ...) custom-call(bf16[256,1536]{1,0:T(8,128)(2,1)} %bitcast.141, ...), custom_call_target="tpu_custom_call" | custom-call | flops 4026531840 | bytes 20971520 | tf_op jit(solution)/shard_map/pallas_call | solution.py:70
  225.0 7.6 %shard_map.353 = (bf16[4,192,1024]{2,1,0:T(8,128)(2,1)}, bf16[4,192,1024]{2,1,0:T(8,128)(2,1)}, bf16[64,1536]{1,0:T(8,128)(2,1)S(1)}, bf16[64,1536]{1,0:T(8,128)...) custom-call(bf16[256,1536]{1,0:T(8,128)(2,1)} %get-tuple-element.92.grad_out, ...), custom_call_target="tpu_custom_call" | custom-call | flops 1610612736 | bytes 15728640 | tf_op jit(solution)/shard_map/pallas_call | solution.py:70
  241.3 3.9 shard_map.361
  246.4 19.4 %collective-permute-done.65 = bf16[64,1536]{1,0:T(8,128)(2,1)S(1)} collective-permute-done((bf16[64,1536]{1,0:T(8,128)(2,1)S(1)}, bf16[64,1536]{1,0:T(8,128)(2,1)S(1)}, u32[]{:S(2)}, u32[]{:S(2)}) %collective-permute-start.65) | collective-permute-done | bytes 196640 | tf_op jit(solution)/shard_map/ppermute | solution.py:655
  268.4 4.3 collective-permute-start.67
  276.2 10.3 %collective-permute-done.67.rest_10_.rest_6_ = bf16[64,1536]{1,0:T(8,128)(2,1)S(1)} collective-permute-done((bf16[64,1536]{1,0:T(8,128)(2,1)S(1)}, bf16[64,1536]{1,0:T(8,128)(2,1)S(1)}, u32[]{:S(2)}, u32[]{:S(2)}) %collective-permute-start.67) | collective-permute-done | bytes 196640 | tf_op jit(solution)/shard_map/ppermute | solution.py:655
  289.9 8.8 %collective-permute-done.68.rest_11_.rest_7_ = bf16[64,1536]{1,0:T(8,128)(2,1)S(1)} collective-permute-done((bf16[64,1536]{1,0:T(8,128)(2,1)S(1)}, bf16[64,1536]{1,0:T(8,128)(2,1)S(1)}, u32[]{:S(2)}, u32[]{:S(2)}) %collective-permute-start.68) | collective-permute-done | bytes 196640 | tf_op jit(solution)/shard_map/ppermute | solution.py:655
  299.1 7.3 %shard_map.355 = (f32[256,1536]{1,0:T(8,128)}, bf16[256,1536]{1,0:T(8,128)(2,1)S(1)}, f32[256,384]{1,0:T(8,128)S(1)}) custom-call(f32[256,1536]{1,0:T(8,128)} %get-tuple-element.91.hidden, bf16[256,12]{1,0:T(8,128)(2,1)S(1)} %copy.72.member, f32[1,1536]{1,0:T(1,128)S(1)} %copy-done.73, bf16[256,1536]{1,0:T(8,128)(2,1)S(1)} %bitcast.138, ...), custom_call_target="tpu_custom_call" | custom-call | flops 301989888 | bytes 8388608 | tf_op jit(solution)/shard_map/pallas_call | solution.py:70
  307.5 27.3 %shard_map.356 = (bf16[256,384]{1,0:T(8,128)(2,1)S(1)}, bf16[256,384]{1,0:T(8,128)(2,1)S(1)}, bf16[256,384]{1,0:T(8,128)(2,1)S(1)}, bf16[12,256,384]{2,1,0:T(8,1...) custom-call(s32[12]{0:T(128)S(1)} %copy-done.82, s32[12]{0:T(128)S(1)} %copy-done.107, ...), custom_call_target="tpu_custom_call" | custom-call | flops 4294967296 | bytes 15728640 | tf_op jit(solution)/shard_map/pallas_call | solution.py:70
  336.2 23.2 %shard_map.360 = (bf16[4,512,384]{2,1,0:T(8,128)(2,1)}, bf16[4,512,384]{2,1,0:T(8,128)(2,1)}) custom-call(s32[12]{0:T(128)} %copy-done.81, s32[12]{0:T(128)} %bitcast.148, s32[1]{0:T(128)} %bitcast.39.rank, bf16[12,256,4096]{2,1,0:T(8,128)(2,1)} %bitcast.151, bf16[12,256,384]{2,1,0:T(8,128)(2,1)} %copy-done.2, ...), custom_call_target="tpu_custom_call" | custom-call | flops 4831838208 | bytes 10485760 | tf_op jit(solution)/shard_map/pallas_call | solution.py:897
  359.4 8.6 %shard_map.357 = (bf16[4,192,768]{2,1,0:T(8,128)(2,1)}, bf16[4,192,768]{2,1,0:T(8,128)(2,1)}, bf16[4,192,768]{2,1,0:T(8,128)(2,1)}, bf16[4,192,768]{2,1,0:T(8,12...) custom-call(bf16[256,1536]{1,0:T(8,128)(2,1)} %get-tuple-element.105, ...), custom_call_target="tpu_custom_call" | custom-call | flops 2113929216 | bytes 15728640 | tf_op jit(solution)/shard_map/pallas_call | solution.py:70
  372.2 23.2 %shard_map.359 = (bf16[4,512,384]{2,1,0:T(8,128)(2,1)}, bf16[4,512,384]{2,1,0:T(8,128)(2,1)}) custom-call(s32[12]{0:T(128)} %copy-done.81, s32[12]{0:T(128)} %bitcast.149, s32[1]{0:T(128)} %bitcast.39.rank, bf16[12,256,4096]{2,1,0:T(8,128)(2,1)} %bitcast.152, bf16[12,256,384]{2,1,0:T(8,128)(2,1)} %copy-done.2, ...), custom_call_target="tpu_custom_call" | custom-call | flops 4831838208 | bytes 10485760 | tf_op jit(solution)/shard_map/pallas_call | solution.py:897
  399.7 3.6 shard_map.354
  405.6 3.7 collective-permute-start.73
  413.2 9.6 %collective-permute-done.73.rest_6_ = bf16[64,1536]{1,0:T(8,128)(2,1)S(1)} collective-permute-done((bf16[64,1536]{1,0:T(8,128)(2,1)S(1)}, bf16[64,1536]{1,0:T(8,128)(2,1)S(1)}, u32[]{:S(2)}, u32[]{:S(2)}) %collective-permute-start.73) | collective-permute-done | bytes 196640 | tf_op jit(solution)/shard_map/ppermute | solution.py:655
  426.2 6.6 %shard_map.358 = (bf16[256,1536]{1,0:T(8,128)(2,1)}, bf16[12,1536]{1,0:T(8,128)(2,1)S(1)}, f32[1,1536]{1,0:T(1,128)S(1)}) custom-call(bf16[256,1536]{1,0:T(8,128)(2,1)S(1)} %bitcast.142, bf16[256,12]{1,0:T(8,128)(2,1)S(1)} %copy.72.member, f32[1,1536]{1,0:T(1,128)S(1)} %copy-done.76, f32[256,1536]{1,0:T(8,128)S(1)} %copy-done.6, ...), custom_call_target="tpu_custom_call" | custom-call | bytes 8388608 | tf_op jit(solution)/shard_map/pallas_call | solution.py:70
  436.8 9.1 %collective-permute-done.103 = f32[4230]{0:T(1024)S(1)} collective-permute-done((f32[4230]{0:T(1024)S(1)}, f32[4230]{0:T(1024)S(1)}, u32[]{:S(2)}, u32[]{:S(2)}) %collective-permute-start.103) | collective-permute-done | bytes 16952 | tf_op jit(solution)/shard_map/ppermute | solution.py:631
  445.9 34.5 %collective-permute-start.97 = (bf16[2,192,512]{2,1,0:T(8,128)(2,1)}, bf16[2,192,512]{2,1,0:T(8,128)(2,1)}, u32[]{:S(2)}, u32[]{:S(2)}) collective-permute-start(bf16[2,192,512]{2,1,0:T(8,128)(2,1)} %pad_maximum_fusion.10), channel_id=1, source_target_pairs={{0,16},{4,20},{8,24},{12,28},{16,0},{20,4},{24,8},{28,12},{1,17},{... | collective-permute-start | bytes 1179656 | tf_op jit(solution)/shard_map/ppermute | solution.py:631
  480.5 9.8 %collective-permute-done.104 = f32[4230]{0:T(1024)S(1)} collective-permute-done((f32[4230]{0:T(1024)S(1)}, f32[4230]{0:T(1024)S(1)}, u32[]{:S(2)}, u32[]{:S(2)}) %collective-permute-start.104) | collective-permute-done | bytes 16952 | tf_op jit(solution)/shard_map/ppermute | solution.py:631
  525.9 24.4 %collective-permute-done.76 = bf16[2,192,768]{2,1,0:T(8,128)(2,1)S(1)} collective-permute-done((bf16[2,192,768]{2,1,0:T(8,128)(2,1)S(1)}, bf16[2,192,768]{2,1,0:T(8,128)(2,1)S(1)}, u32[]{:S(2)}, u32[]{:S(2)}) %collective-permute-start.76) | collective-permute-done | bytes 589856 | tf_op jit(solution)/shard_map/ppermute | solution.py:631
  558.3 18.9 %collective-permute-done.77 = bf16[192,768]{1,0:T(8,128)(2,1)S(1)} collective-permute-done((bf16[192,768]{1,0:T(8,128)(2,1)S(1)}, bf16[192,768]{1,0:T(8,128)(2,1)S(1)}, u32[]{:S(2)}, u32[]{:S(2)}) %collective-permute-start.77) | collective-permute-done | bytes 294944 | tf_op jit(solution)/shard_map/ppermute | solution.py:631
  (645 shorter events, 220.8 us)
Async XLA Ops:
  2.7 28.2 %collective-permute-start.10 = (bf16[192,768]{1,0:T(8,128)(2,1)S(1)}, bf16[192,768]{1,0:T(8,128)(2,1)S(1)}, u32[]{:S(2)}, u32[]{:S(2)}) collective-permute-start(bf16[192,768]{1,0:T(8,128)(2,1)S(1)} %constant_dynamic-update-slice_fusion.rest_4_.rest_0_), channel_id=1, source_target_pairs={{0,8},{4,12},{8,0},{12,4},{16,24},{20,28},{24,16},{28,20},{1,9},{5... | collective-permute-start | bytes 884744 | tf_op jit(solution)/shard_map/ppermute | solution.py:631
  108.4 28.4 %collective-permute-start.36 = (bf16[512,384]{1,0:T(8,128)(2,1)}, bf16[512,384]{1,0:T(8,128)(2,1)}, u32[]{:S(2)}, u32[]{:S(2)}) collective-permute-start(bf16[512,384]{1,0:T(8,128)(2,1)} %collective-permute-done.35.rest_14_), channel_id=1, source_target_pairs={{0,4},{4,0},{8,12},{12,8},{16,20},{20,16},{24,28},{28,24},{1,5},{5... | collective-permute-start | bytes 1179656 | tf_op jit(solution)/shard_map/ppermute | solution.py:631
  134.2 40.4 %collective-permute-start.50 = (bf16[192,1536]{1,0:T(8,128)(2,1)S(1)}, bf16[192,1536]{1,0:T(8,128)(2,1)S(1)}, u32[]{:S(2)}, u32[]{:S(2)}) collective-permute-start(bf16[192,1536]{1,0:T(8,128)(2,1)S(1)} %copy-done.115), channel_id=1, source_target_pairs={{0,4},{4,0},{8,12},{12,8},{16,20},{20,16},{24,28},{28,24},{1,5},{5... | collective-permute-start | bytes 1769480 | tf_op jit(solution)/shard_map/ppermute | solution.py:631
  134.7 41.4 %collective-permute-start.53 = (bf16[192,1536]{1,0:T(8,128)(2,1)S(1)}, bf16[192,1536]{1,0:T(8,128)(2,1)S(1)}, u32[]{:S(2)}, u32[]{:S(2)}) collective-permute-start(bf16[192,1536]{1,0:T(8,128)(2,1)S(1)} %copy-done.115), channel_id=1, source_target_pairs={{0,16},{4,20},{8,24},{12,28},{16,0},{20,4},{24,8},{28,12},{1,17},{... | collective-permute-start | bytes 1769480 | tf_op jit(solution)/shard_map/ppermute | solution.py:631
  135.7 42.4 %collective-permute-start.45 = (bf16[192,1536]{1,0:T(8,128)(2,1)S(1)}, bf16[192,1536]{1,0:T(8,128)(2,1)S(1)}, u32[]{:S(2)}, u32[]{:S(2)}) collective-permute-start(bf16[192,1536]{1,0:T(8,128)(2,1)S(1)} %copy-done.39), channel_id=1, source_target_pairs={{0,4},{4,0},{8,12},{12,8},{16,20},{20,16},{24,28},{28,24},{1,5},{5... | collective-permute-start | bytes 1769480 | tf_op jit(solution)/shard_map/ppermute | solution.py:631
  135.7 42.5 %collective-permute-start.48 = (bf16[192,1536]{1,0:T(8,128)(2,1)S(1)}, bf16[192,1536]{1,0:T(8,128)(2,1)}, u32[]{:S(2)}, u32[]{:S(2)}) collective-permute-start(bf16[192,1536]{1,0:T(8,128)(2,1)S(1)} %copy-done.42), channel_id=1, source_target_pairs={{0,8},{4,12},{8,0},{12,4},{16,24},{20,28},{24,16},{28,20},{1,9},{5... | collective-permute-start | bytes 1769480 | tf_op jit(solution)/shard_map/ppermute | solution.py:631
  136.8 41.6 %collective-permute-start.55 = (bf16[192,1536]{1,0:T(8,128)(2,1)S(1)}, bf16[192,1536]{1,0:T(8,128)(2,1)}, u32[]{:S(2)}, u32[]{:S(2)}) collective-permute-start(bf16[192,1536]{1,0:T(8,128)(2,1)S(1)} %copy-done.127), channel_id=1, source_target_pairs={{0,16},{4,20},{8,24},{12,28},{16,0},{20,4},{24,8},{28,12},{1,17},{... | collective-permute-start | bytes 1769480 | tf_op jit(solution)/shard_map/ppermute | solution.py:631
  232.6 33.8 %collective-permute-start.59 = (bf16[64,1536]{1,0:T(8,128)(2,1)S(1)}, bf16[64,1536]{1,0:T(8,128)(2,1)S(1)}, u32[]{:S(2)}, u32[]{:S(2)}) collective-permute-start(bf16[64,1536]{1,0:T(8,128)(2,1)S(1)} %get-tuple-element.97), channel_id=1, source_target_pairs={{0,3},{1,0},{2,1},{3,2},{4,7},{5,4},{6,5},{7,6},{8,11},{9,8},{10,9... | collective-permute-start | bytes 589832 | tf_op jit(solution)/shard_map/ppermute | solution.py:655
  232.7 35.7 %collective-permute-start.58 = (bf16[64,1536]{1,0:T(8,128)(2,1)S(1)}, bf16[64,1536]{1,0:T(8,128)(2,1)S(1)}, u32[]{:S(2)}, u32[]{:S(2)}) collective-permute-start(bf16[64,1536]{1,0:T(8,128)(2,1)S(1)} %get-tuple-element.96), channel_id=1, source_target_pairs={{0,2},{1,3},{2,0},{3,1},{4,6},{5,7},{6,4},{7,5},{8,10},{9,11},{10,... | collective-permute-start | bytes 589832 | tf_op jit(solution)/shard_map/ppermute | solution.py:655
  233.6 32.2 %collective-permute-start.65 = (bf16[64,1536]{1,0:T(8,128)(2,1)S(1)}, bf16[64,1536]{1,0:T(8,128)(2,1)S(1)}, u32[]{:S(2)}, u32[]{:S(2)}) collective-permute-start(bf16[64,1536]{1,0:T(8,128)(2,1)S(1)} %get-tuple-element.101), channel_id=1, source_target_pairs={{0,3},{1,0},{2,1},{3,2},{4,7},{5,4},{6,5},{7,6},{8,11},{9,8},{10,9... | collective-permute-start | bytes 589832 | tf_op jit(solution)/shard_map/ppermute | solution.py:655
  236.2 29.6 %collective-permute-start.64 = (bf16[64,1536]{1,0:T(8,128)(2,1)S(1)}, bf16[64,1536]{1,0:T(8,128)(2,1)S(1)}, u32[]{:S(2)}, u32[]{:S(2)}) collective-permute-start(bf16[64,1536]{1,0:T(8,128)(2,1)S(1)} %get-tuple-element.100), channel_id=1, source_target_pairs={{0,2},{1,3},{2,0},{3,1},{4,6},{5,7},{6,4},{7,5},{8,10},{9,11},{10,... | collective-permute-start | bytes 589832 | tf_op jit(solution)/shard_map/ppermute | solution.py:655
  237.9 27.9 %collective-permute-start.63 = (bf16[64,1536]{1,0:T(8,128)(2,1)S(1)}, bf16[64,1536]{1,0:T(8,128)(2,1)S(1)}, u32[]{:S(2)}, u32[]{:S(2)}) collective-permute-start(bf16[64,1536]{1,0:T(8,128)(2,1)S(1)} %get-tuple-element.99), channel_id=1, source_target_pairs={{0,1},{1,2},{2,3},{3,0},{4,5},{5,6},{6,7},{7,4},{8,9},{9,10},{10,1... | collective-permute-start | bytes 589832 | tf_op jit(solution)/shard_map/ppermute | solution.py:655
  265.8 139.8 %collective-permute-start.93 = (bf16[4,192,512]{2,1,0:T(8,128)(2,1)}, bf16[4,192,512]{2,1,0:T(8,128)(2,1)}, u32[]{:S(2)}, u32[]{:S(2)}) collective-permute-start(bf16[4,192,512]{2,1,0:T(8,128)(2,1)} %get-tuple-element.174), channel_id=1, source_target_pairs={{0,4},{4,0},{8,12},{12,8},{16,20},{20,16},{24,28},{28,24},{1,5},{5... | collective-permute-start | bytes 2359304 | tf_op jit(solution)/shard_map/ppermute | solution.py:631
  265.8 143.4 %collective-permute-start.96 = (bf16[4,192,512]{2,1,0:T(8,128)(2,1)}, bf16[4,192,512]{2,1,0:T(8,128)(2,1)}, u32[]{:S(2)}, u32[]{:S(2)}) collective-permute-start(bf16[4,192,512]{2,1,0:T(8,128)(2,1)} %get-tuple-element.175), channel_id=1, source_target_pairs={{0,4},{4,0},{8,12},{12,8},{16,20},{20,16},{24,28},{28,24},{1,5},{5... | collective-permute-start | bytes 2359304 | tf_op jit(solution)/shard_map/ppermute | solution.py:631
  276.0 92.0 %collective-permute-start.60 = (bf16[64,1536]{1,0:T(8,128)(2,1)S(1)}, bf16[64,1536]{1,0:T(8,128)(2,1)S(1)}, u32[]{:S(2)}, u32[]{:S(2)}) collective-permute-start(bf16[64,1536]{1,0:T(8,128)(2,1)S(1)} %add_convert_fusion.26.rest_4_), channel_id=1, source_target_pairs={{0,1},{1,2},{2,3},{3,0},{4,5},{5,6},{6,7},{7,4},{8,9},{9,10},{10,1... | collective-permute-start | bytes 589832 | tf_op jit(solution)/shard_map/ppermute | solution.py:655
  286.5 81.6 %collective-permute-start.61 = (bf16[64,1536]{1,0:T(8,128)(2,1)S(1)}, bf16[64,1536]{1,0:T(8,128)(2,1)S(1)}, u32[]{:S(2)}, u32[]{:S(2)}) collective-permute-start(bf16[64,1536]{1,0:T(8,128)(2,1)S(1)} %add_convert_fusion.26.rest_4_), channel_id=1, source_target_pairs={{0,2},{1,3},{2,0},{3,1},{4,6},{5,7},{6,4},{7,5},{8,10},{9,11},{10,... | collective-permute-start | bytes 589832 | tf_op jit(solution)/shard_map/ppermute | solution.py:655
  298.7 72.9 %collective-permute-start.62 = (bf16[64,1536]{1,0:T(8,128)(2,1)S(1)}, bf16[64,1536]{1,0:T(8,128)(2,1)S(1)}, u32[]{:S(2)}, u32[]{:S(2)}) collective-permute-start(bf16[64,1536]{1,0:T(8,128)(2,1)S(1)} %add_convert_fusion.26.rest_4_), channel_id=1, source_target_pairs={{0,3},{1,0},{2,1},{3,2},{4,7},{5,4},{6,5},{7,6},{8,11},{9,8},{10,9... | collective-permute-start | bytes 589832 | tf_op jit(solution)/shard_map/ppermute | solution.py:655
  368.1 35.2 %collective-permute-start.71 = (bf16[64,1536]{1,0:T(8,128)(2,1)}, bf16[64,1536]{1,0:T(8,128)(2,1)}, u32[]{:S(2)}, u32[]{:S(2)}) collective-permute-start(bf16[64,1536]{1,0:T(8,128)(2,1)} %get-tuple-element.119), channel_id=1, source_target_pairs={{0,3},{1,0},{2,1},{3,2},{4,7},{5,4},{6,5},{7,6},{8,11},{9,8},{10,9... | collective-permute-start | bytes 589832 | tf_op jit(solution)/shard_map/ppermute | solution.py:655
  368.2 35.2 %collective-permute-start.70 = (bf16[64,1536]{1,0:T(8,128)(2,1)}, bf16[64,1536]{1,0:T(8,128)(2,1)}, u32[]{:S(2)}, u32[]{:S(2)}) collective-permute-start(bf16[64,1536]{1,0:T(8,128)(2,1)} %get-tuple-element.118), channel_id=1, source_target_pairs={{0,2},{1,3},{2,0},{3,1},{4,6},{5,7},{6,4},{7,5},{8,10},{9,11},{10,... | collective-permute-start | bytes 589832 | tf_op jit(solution)/shard_map/ppermute | solution.py:655
  371.7 32.2 %collective-permute-start.69 = (bf16[64,1536]{1,0:T(8,128)(2,1)}, bf16[64,1536]{1,0:T(8,128)(2,1)}, u32[]{:S(2)}, u32[]{:S(2)}) collective-permute-start(bf16[64,1536]{1,0:T(8,128)(2,1)} %get-tuple-element.117), channel_id=1, source_target_pairs={{0,1},{1,2},{2,3},{3,0},{4,5},{5,6},{6,7},{7,4},{8,9},{9,10},{10,1... | collective-permute-start | bytes 589832 | tf_op jit(solution)/shard_map/ppermute | solution.py:655
  403.3 112.0 %collective-permute-start.87 = (bf16[4,192,1024]{2,1,0:T(8,128)(2,1)}, bf16[4,192,1024]{2,1,0:T(8,128)(2,1)}, u32[]{:S(2)}, u32[]{:S(2)}) collective-permute-start(bf16[4,192,1024]{2,1,0:T(8,128)(2,1)} %copy-done.90), channel_id=1, source_target_pairs={{0,4},{4,0},{8,12},{12,8},{16,20},{20,16},{24,28},{28,24},{1,5},{5... | collective-permute-start | bytes 4718600 | tf_op jit(solution)/shard_map/ppermute | solution.py:631
  403.4 113.9 %collective-permute-start.90 = (bf16[4,192,1024]{2,1,0:T(8,128)(2,1)}, bf16[4,192,1024]{2,1,0:T(8,128)(2,1)}, u32[]{:S(2)}, u32[]{:S(2)}) collective-permute-start(bf16[4,192,1024]{2,1,0:T(8,128)(2,1)} %get-tuple-element.137), channel_id=1, source_target_pairs={{0,4},{4,0},{8,12},{12,8},{16,20},{20,16},{24,28},{28,24},{1,5},{5... | collective-permute-start | bytes 4718600 | tf_op jit(solution)/shard_map/ppermute | solution.py:631
  433.7 68.7 %collective-permute-start.94 = (bf16[2,192,512]{2,1,0:T(8,128)(2,1)}, bf16[2,192,512]{2,1,0:T(8,128)(2,1)}, u32[]{:S(2)}, u32[]{:S(2)}) collective-permute-start(bf16[2,192,512]{2,1,0:T(8,128)(2,1)} %pad_maximum_fusion.9), channel_id=1, source_target_pairs={{0,8},{4,12},{8,0},{12,4},{16,24},{20,28},{24,16},{28,20},{1,9},{5... | collective-permute-start | bytes 1179656 | tf_op jit(solution)/shard_map/ppermute | solution.py:631
  433.7 46.7 %collective-permute-start.99 = (bf16[1,12,1536]{2,1,0:T(8,128)(2,1)S(1)}, bf16[1,12,1536]{2,1,0:T(8,128)(2,1)S(1)}, u32[]{:S(2)}, u32[]{:S(2)}) collective-permute-start(bf16[1,12,1536]{2,1,0:T(8,128)(2,1)S(1)} %bitcast.143), channel_id=1, source_target_pairs={{0,4},{4,0},{8,12},{12,8},{16,20},{20,16},{24,28},{28,24},{1,5},{5... | collective-permute-start | bytes 110600 | tf_op jit(solution)/shard_map/ppermute | solution.py:631
  445.9 56.6 %collective-permute-start.97 = (bf16[2,192,512]{2,1,0:T(8,128)(2,1)}, bf16[2,192,512]{2,1,0:T(8,128)(2,1)}, u32[]{:S(2)}, u32[]{:S(2)}) collective-permute-start(bf16[2,192,512]{2,1,0:T(8,128)(2,1)} %pad_maximum_fusion.10), channel_id=1, source_target_pairs={{0,16},{4,20},{8,24},{12,28},{16,0},{20,4},{24,8},{28,12},{1,17},{... | collective-permute-start | bytes 1179656 | tf_op jit(solution)/shard_map/ppermute | solution.py:631
  517.3 37.0 %collective-permute-start.88 = (bf16[2,192,1024]{2,1,0:T(8,128)(2,1)S(1)}, bf16[2,192,1024]{2,1,0:T(8,128)(2,1)S(1)}, u32[]{:S(2)}, u32[]{:S(2)}) collective-permute-start(bf16[2,192,1024]{2,1,0:T(8,128)(2,1)S(1)} %pad_maximum_fusion.2), channel_id=1, source_target_pairs={{0,8},{4,12},{8,0},{12,4},{16,24},{20,28},{24,16},{28,20},{1,9},{5... | collective-permute-start | bytes 2359304 | tf_op jit(solution)/shard_map/ppermute | solution.py:631
  520.6 35.0 %collective-permute-start.91 = (bf16[2,192,1024]{2,1,0:T(8,128)(2,1)S(1)}, bf16[2,192,1024]{2,1,0:T(8,128)(2,1)S(1)}, u32[]{:S(2)}, u32[]{:S(2)}) collective-permute-start(bf16[2,192,1024]{2,1,0:T(8,128)(2,1)S(1)} %pad_maximum_fusion.3), channel_id=1, source_target_pairs={{0,16},{4,20},{8,24},{12,28},{16,0},{20,4},{24,8},{28,12},{1,17},{... | collective-permute-start | bytes 2359304 | tf_op jit(solution)/shard_map/ppermute | solution.py:631
  521.5 28.9 %collective-permute-start.76 = (bf16[2,192,768]{2,1,0:T(8,128)(2,1)S(1)}, bf16[2,192,768]{2,1,0:T(8,128)(2,1)S(1)}, u32[]{:S(2)}, u32[]{:S(2)}) collective-permute-start(bf16[2,192,768]{2,1,0:T(8,128)(2,1)S(1)} %pad_maximum_fusion.7), channel_id=1, source_target_pairs={{0,8},{4,12},{8,0},{12,4},{16,24},{20,28},{24,16},{28,20},{1,9},{5... | collective-permute-start | bytes 1769480 | tf_op jit(solution)/shard_map/ppermute | solution.py:631
  522.2 31.4 %collective-permute-start.79 = (bf16[2,192,768]{2,1,0:T(8,128)(2,1)S(1)}, bf16[2,192,768]{2,1,0:T(8,128)(2,1)S(1)}, u32[]{:S(2)}, u32[]{:S(2)}) collective-permute-start(bf16[2,192,768]{2,1,0:T(8,128)(2,1)S(1)} %pad_maximum_fusion.8), channel_id=1, source_target_pairs={{0,16},{4,20},{8,24},{12,28},{16,0},{20,4},{24,8},{28,12},{1,17},{... | collective-permute-start | bytes 1769480 | tf_op jit(solution)/shard_map/ppermute | solution.py:631
  524.0 56.8 %collective-permute-start.82 = (bf16[2,512,384]{2,1,0:T(8,128)(2,1)S(1)}, bf16[2,512,384]{2,1,0:T(8,128)(2,1)S(1)}, u32[]{:S(2)}, u32[]{:S(2)}) collective-permute-start(bf16[2,512,384]{2,1,0:T(8,128)(2,1)S(1)} %pad_maximum_fusion), channel_id=1, source_target_pairs={{0,8},{4,12},{8,0},{12,4},{16,24},{20,28},{24,16},{28,20},{1,9},{5... | collective-permute-start | bytes 2359304 | tf_op jit(solution)/shard_map/ppermute | solution.py:631
  550.4 31.2 %collective-permute-start.85 = (bf16[2,512,384]{2,1,0:T(8,128)(2,1)S(1)}, bf16[2,512,384]{2,1,0:T(8,128)(2,1)S(1)}, u32[]{:S(2)}, u32[]{:S(2)}) collective-permute-start(bf16[2,512,384]{2,1,0:T(8,128)(2,1)S(1)} %pad_maximum_fusion.1), channel_id=1, source_target_pairs={{0,16},{4,20},{8,24},{12,28},{16,0},{20,4},{24,8},{28,12},{1,17},{... | collective-permute-start | bytes 2359304 | tf_op jit(solution)/shard_map/ppermute | solution.py:631
  555.6 30.0 %collective-permute-start.89 = (bf16[192,1024]{1,0:T(8,128)(2,1)S(1)}, bf16[192,1024]{1,0:T(8,128)(2,1)S(1)}, u32[]{:S(2)}, u32[]{:S(2)}) collective-permute-start(bf16[192,1024]{1,0:T(8,128)(2,1)S(1)} %fusion.2), channel_id=1, source_target_pairs={{0,16},{4,20},{8,24},{12,28},{16,0},{20,4},{24,8},{28,12},{1,17},{... | collective-permute-start | bytes 1179656 | tf_op jit(solution)/shard_map/ppermute | solution.py:631
  (217 other events, 4139.4 us)
